TPU v7x, 128 devices: a whole 4x4x4 slice. The times are simulated.
128 devices in a mesh: lat: 8 (over y, z_lo), lon: 16 (over z_hi, x, core).
Axes of the slice: x: 4, y: 4, z: 4 (z_hi: 2, z_lo: 2; z = z_hi * 2 + z_lo), core: 2. Of those that a mesh axis runs over, the one named last changes fastest.
Arguments:
- tokens: bfloat16 [224, 448, 4, 256], P('lat', 'lon'), may hold values from -36 to 36
- out_grad: bfloat16 [224, 448, 4, 256], P('lat', 'lon'), may hold values from -6 to 6
- gains: float32 [2, 256], replicated, may hold values from 0.25 to 1.75
- shifts: float32 [2, 256], replicated, may hold values from -3 to 3
- w_qkv: bfloat16 [256, 768], replicated, may hold values from -0.375 to 0.375
- b_qkv: float32 [768], replicated, may hold values from -3 to 3
- w_proj: bfloat16 [256, 256], replicated, may hold values from -0.375 to 0.375
- w_in: bfloat16 [256, 1024], replicated, may hold values from -0.375 to 0.375
- w_out: bfloat16 [1024, 256], replicated, may hold values from -0.1875 to 0.1875
- rel_bias: float32 [8, 507], replicated, may hold values from -4 to 320
Outputs:
- result: bfloat16 [224, 448, 4, 256], P('lat', 'lon')
- in_grad: bfloat16 [224, 448, 4, 256], P('lat', 'lon')
- grad_gains: float32 [2, 256], replicated
- grad_shifts: float32 [2, 256], replicated
- grad_w_qkv: float32 [256, 768], replicated
- grad_b_qkv: float32 [768], replicated
- grad_w_proj: float32 [256, 256], replicated
- grad_w_in: float32 [256, 1024], replicated
- grad_w_out: float32 [1024, 256], replicated
- grad_rel_bias: float32 [8, 507], replicated
All inputs are finite; a program needn't handle non-finite values.
Results may differ from a plain program's by a relative error of at most 0.012.
Values may be sent and summed in bfloat16 or wider, within the bound.
A program may use at most 192 MiB of HBM per device.

v0:
```python
import jax
import jax.numpy as jnp
from jax import lax
from jax.sharding import PartitionSpec as P

WIN = 7
LEV = 4
WLEV = 2
SHIFT = 3


EPSILON = 1e-05
NEG_LARGE = -1e30


def shifted(value, axis, steps):
    count = lax.axis_size(axis)
    pairs = [(source, (source + steps) % count) for source in range(count)]
    return lax.ppermute(value, axis, pairs)


def norm_forward(values, gain, offset):
    center = values - jnp.mean(values, -1, keepdims=True)
    variance = jnp.mean(center * center, -1, keepdims=True)
    inv_std = lax.rsqrt(variance + EPSILON)
    normed = center * inv_std
    return (normed, inv_std, (normed * gain + offset).astype(jnp.bfloat16))


def norm_backward(upstream, normed, inv_std, gain):
    scaled = upstream * gain
    return inv_std * (
        scaled
        - jnp.mean(scaled, -1, keepdims=True)
        - normed * jnp.mean(scaled * normed, -1, keepdims=True)
    )


def relative_table(width_tok, rel_count):
    positions = jnp.arange(width_tok, dtype=jnp.int32)
    lat_pos = positions // (WIN * WLEV)
    lon_pos = positions // WLEV % WIN
    lev_pos = positions % WLEV
    offsets = (
        (
            (lat_pos[:, None] - lat_pos[None, :] + WIN - 1) * (2 * WIN - 1)
            + lon_pos[:, None]
            - lon_pos[None, :]
            + WIN
            - 1
        )
        * (2 * WLEV - 1)
        + lev_pos[:, None]
        - lev_pos[None, :]
        + WLEV
        - 1
    )
    return (offsets.reshape(-1)[:, None] == jnp.arange(rel_count, dtype=jnp.int32)[None, :]).astype(
        jnp.float32
    )


def to_windows(block):
    rows_n, cols_n, levels, channels = block.shape
    tiled = block.reshape(rows_n // WIN, WIN, cols_n // WIN, WIN, levels // WLEV, WLEV, channels)
    return tiled.transpose(0, 2, 4, 1, 3, 5, 6).reshape(-1, WIN * WIN * WLEV, channels)


def from_windows(windows, rows_n, cols_n):
    channels = windows.shape[-1]
    tiled = windows.reshape(rows_n // WIN, cols_n // WIN, LEV // WLEV, WIN, WIN, WLEV, channels)
    return tiled.transpose(0, 3, 1, 4, 2, 5, 6).reshape(rows_n, cols_n, LEV, channels)


def roll_in(stacked):
    got_cols = shifted(stacked[:, :, :SHIFT], "lon", -1)
    widened = jnp.concatenate([stacked[:, :, SHIFT:], got_cols], 2)
    got_rows = shifted(widened[:, :SHIFT], "lat", -1)
    return jnp.concatenate([widened[:, SHIFT:], got_rows], 1)


def roll_out(stacked):
    got_rows = shifted(stacked[:, -SHIFT:], "lat", 1)
    settled = jnp.concatenate([got_rows, stacked[:, :-SHIFT]], 1)
    got_cols = shifted(settled[:, :, -SHIFT:], "lon", 1)
    return jnp.concatenate([got_cols, settled[:, :, :-SHIFT]], 2)


def forward(windows, allowed, onehot, params):
    gains, shifts, w_qkv, b_qkv, w_proj, w_in, w_out, rel_bias = params
    count, width_tok, channels = windows.shape
    heads = rel_bias.shape[0]
    head_dim = channels // heads
    flat = windows.reshape(count * width_tok, channels).astype(jnp.float32)
    normed1, inv_std1, hidden1 = norm_forward(flat, gains[0], shifts[0])
    projected = (jnp.dot(hidden1, w_qkv, preferred_element_type=jnp.float32) + b_qkv).astype(
        jnp.bfloat16
    )
    projected = projected.reshape(count, width_tok, 3, heads, head_dim)
    queries = projected[:, :, 0]
    keys_in = projected[:, :, 1]
    values_in = projected[:, :, 2]
    bias_full = jnp.dot(rel_bias, onehot.T, precision=lax.Precision.HIGHEST).reshape(
        heads, width_tok, width_tok
    )
    scores = (
        jnp.einsum("bqhd,bkhd->bhqk", queries, keys_in, preferred_element_type=jnp.float32)
        * head_dim ** (-0.5)
        + bias_full[None]
    )
    scores = jnp.where(allowed[:, None], scores, NEG_LARGE)
    highest = jnp.max(scores, -1, keepdims=True)
    weights_raw = jnp.exp(scores - highest)
    attention = weights_raw / jnp.sum(weights_raw, -1, keepdims=True)
    attention_low = attention.astype(jnp.bfloat16)
    mixed = jnp.einsum(
        "bhqk,bkhd->bqhd", attention_low, values_in, preferred_element_type=jnp.float32
    )
    mixed = mixed.astype(jnp.bfloat16).reshape(count * width_tok, channels)
    residual = flat + jnp.dot(mixed, w_proj, preferred_element_type=jnp.float32)
    normed2, inv_std2, hidden2 = norm_forward(residual, gains[1], shifts[1])
    pre_gelu = jnp.dot(hidden2, w_in, preferred_element_type=jnp.float32)
    activated = jax.nn.gelu(pre_gelu).astype(jnp.bfloat16)
    block_out = (residual + jnp.dot(activated, w_out, preferred_element_type=jnp.float32)).astype(
        jnp.bfloat16
    )
    saved = (
        normed1,
        inv_std1,
        hidden1,
        queries,
        keys_in,
        values_in,
        attention,
        attention_low,
        mixed,
        normed2,
        inv_std2,
        hidden2,
        pre_gelu,
        activated,
    )
    return (block_out.reshape(count, width_tok, channels), saved)


def mlp_backward(grad_windows, saved, params):
    gains, shifts, w_qkv, b_qkv, w_proj, w_in, w_out, rel_bias = params
    normed2, inv_std2, hidden2, pre_gelu, activated = (
        saved[9],
        saved[10],
        saved[11],
        saved[12],
        saved[13],
    )
    grad_low = grad_windows.reshape(-1, grad_windows.shape[-1])
    grad_w_out = jnp.dot(activated.T, grad_low, preferred_element_type=jnp.float32)
    grad_act = jnp.dot(grad_low, w_out.T, preferred_element_type=jnp.float32)
    unused, pullback = jax.vjp(jax.nn.gelu, pre_gelu)
    grad_pre = pullback(grad_act)[0].astype(jnp.bfloat16)
    grad_w_in = jnp.dot(hidden2.T, grad_pre, preferred_element_type=jnp.float32)
    grad_hidden2 = jnp.dot(grad_pre, w_in.T, preferred_element_type=jnp.float32)
    grad_gain2 = jnp.sum(grad_hidden2 * normed2, 0)
    grad_shift2 = jnp.sum(grad_hidden2, 0)
    grad_resid = grad_low.astype(jnp.float32) + norm_backward(
        grad_hidden2, normed2, inv_std2, gains[1]
    )
    return (grad_resid, (grad_w_in, grad_w_out, grad_gain2, grad_shift2))


def attention_backward(grad_resid, saved, params, onehot):
    gains, shifts, w_qkv, b_qkv, w_proj, w_in, w_out, rel_bias = params
    normed1, inv_std1, hidden1, queries, keys_in, values_in, attention, attention_low, mixed = (
        saved[:9]
    )
    count, width_tok, heads, head_dim = queries.shape
    channels = heads * head_dim
    grad_low = grad_resid.astype(jnp.bfloat16)
    grad_w_proj = jnp.dot(mixed.T, grad_low, preferred_element_type=jnp.float32)
    grad_mixed = jnp.dot(grad_low, w_proj.T, preferred_element_type=jnp.float32).astype(
        jnp.bfloat16
    )
    grad_mixed = grad_mixed.reshape(count, width_tok, heads, head_dim)
    grad_attn = jnp.einsum(
        "bqhd,bkhd->bhqk", grad_mixed, values_in, preferred_element_type=jnp.float32
    )
    grad_values = jnp.einsum(
        "bhqk,bqhd->bkhd", attention_low, grad_mixed, preferred_element_type=jnp.float32
    ).astype(jnp.bfloat16)
    grad_scores = attention * (grad_attn - jnp.sum(grad_attn * attention, -1, keepdims=True))
    grad_bias = jnp.sum(grad_scores, 0).reshape(heads, width_tok * width_tok)
    grad_table = jnp.dot(grad_bias, onehot, precision=lax.Precision.HIGHEST)
    grad_scaled = (grad_scores * head_dim ** (-0.5)).astype(jnp.bfloat16)
    grad_queries = jnp.einsum(
        "bhqk,bkhd->bqhd", grad_scaled, keys_in, preferred_element_type=jnp.float32
    ).astype(jnp.bfloat16)
    grad_keys = jnp.einsum(
        "bhqk,bqhd->bkhd", grad_scaled, queries, preferred_element_type=jnp.float32
    ).astype(jnp.bfloat16)
    grad_proj = jnp.stack([grad_queries, grad_keys, grad_values], 2).reshape(
        count * width_tok, 3 * channels
    )
    grad_w_qkv = jnp.dot(hidden1.T, grad_proj, preferred_element_type=jnp.float32)
    grad_b_qkv = jnp.sum(grad_proj, 0, dtype=jnp.float32)
    grad_hidden1 = jnp.dot(grad_proj, w_qkv.T, preferred_element_type=jnp.float32)
    grad_gain1 = jnp.sum(grad_hidden1 * normed1, 0)
    grad_shift1 = jnp.sum(grad_hidden1, 0)
    grad_input = (grad_resid + norm_backward(grad_hidden1, normed1, inv_std1, gains[0])).astype(
        jnp.bfloat16
    )
    return (
        grad_input.reshape(count, width_tok, channels),
        (grad_w_qkv, grad_b_qkv, grad_w_proj, grad_gain1, grad_shift1, grad_table),
    )


def local(tokens, out_grad, gains, shifts, w_qkv, b_qkv, w_proj, w_in, w_out, rel_bias):
    params = (gains, shifts, w_qkv, b_qkv, w_proj, w_in, w_out, rel_bias)
    rows_n, cols_n, levels, channels = tokens.shape
    total_rows = rows_n * lax.axis_size("lat")
    total_tokens = total_rows * cols_n * lax.axis_size("lon") * levels
    width_tok = WIN * WIN * WLEV
    onehot = relative_table(width_tok, rel_bias.shape[1])
    row_global = lax.axis_index("lat") * rows_n + jnp.arange(rows_n, dtype=jnp.int32)
    band_rows = row_global.reshape(rows_n // WIN, WIN)
    group_tok = jnp.repeat(band_rows >= total_rows - SHIFT, WIN * WLEV, axis=1)
    group_win = jnp.repeat(group_tok, cols_n // WIN * (levels // WLEV), axis=0)
    allowed = group_win[:, :, None] == group_win[:, None, :]
    tokens_rolled = roll_in(tokens[None])[0]
    block_out, saved = forward(to_windows(tokens_rolled), allowed, onehot, params)
    result = roll_out(from_windows(block_out, rows_n, cols_n)[None])[0]
    grad_rolled = roll_in(out_grad[None])[0]
    grad_resid, mlp_terms = mlp_backward(to_windows(grad_rolled), saved, params)
    grad_w_in, grad_w_out, grad_gain2, grad_shift2 = mlp_terms
    grad_input, attn_terms = attention_backward(grad_resid, saved, params, onehot)
    grad_w_qkv, grad_b_qkv, grad_w_proj, grad_gain1, grad_shift1, grad_table = attn_terms
    (
        grad_w_in,
        grad_w_out,
        grad_gain2,
        grad_shift2,
        grad_w_qkv,
        grad_b_qkv,
        grad_w_proj,
        grad_gain1,
        grad_shift1,
        grad_table,
    ) = lax.psum(
        (
            grad_w_in,
            grad_w_out,
            grad_gain2,
            grad_shift2,
            grad_w_qkv,
            grad_b_qkv,
            grad_w_proj,
            grad_gain1,
            grad_shift1,
            grad_table,
        ),
        ("lat", "lon"),
    )
    grad_block = from_windows(grad_input, rows_n, cols_n)
    in_grad = roll_out(grad_block[None])[0]
    scale = float(total_tokens) ** (-0.5)
    return (
        result,
        in_grad,
        jnp.stack([grad_gain1, grad_gain2]) * scale,
        jnp.stack([grad_shift1, grad_shift2]) * scale,
        grad_w_qkv * scale,
        grad_b_qkv * scale,
        grad_w_proj * scale,
        grad_w_in * scale,
        grad_w_out * scale,
        grad_table * scale,
    )


def solution(mesh):
    return jax.shard_map(
        local,
        mesh=mesh,
        in_specs=(
            P("lat", "lon", None, None),
            P("lat", "lon", None, None),
            P(),
            P(),
            P(),
            P(),
            P(),
            P(),
            P(),
            P(),
        ),
        out_specs=(
            P("lat", "lon", None, None),
            P("lat", "lon", None, None),
            P(),
            P(),
            P(),
            P(),
            P(),
            P(),
            P(),
            P(),
        ),
        check_vma=False,
    )
```

profile of v0, /device:TPU:1, one launch (start us, length us, event | category | flops | bytes accessed | tf_op | source)
XLA Modules:
  0.0 550.8 jit_solution(510846086923338623)
XLA Ops:
  12.0 5.6 %collective-permute-start = (bf16[1,28,3,4,256]{4,3,2,1,0:T(4,128)(2,1)}, bf16[1,28,3,4,256]{4,3,2,1,0:T(4,128)(2,1)}, u32[]{:S(2)}, u32[]{:S(2)}) collective-permute-start(bf16[1,28,3,4,256]{4,3,2,1,0:T(4,128)(2,1)} %slice.95), channel_id=1, source_target_pairs={{0,15},{1,0},{2,1},{3,2},{4,3},{5,4},{6,5},{7,6},{8,7},{9,8},{10,9... | collective-permute-start | bytes 516104 | tf_op jit(solution)/shard_map/ppermute | solution.py:19
  20.2 10.3 %fusion.15 = f32[8,9604]{1,0:T(8,128)} fusion(f32[8,507]{1,0:T(8,128)} %param.19, s32[9604]{0:T(1024)S(1)} %reshape.283), kind=kOutput, calls=%fused_computation.23 | convolution fusion | flops 472315136 | bytes 361968 | tf_op jit(solution)/shard_map/dot_general | solution.py:103
  83.5 7.7 %add_convert_fusion.1 = bf16[4,4,2,7,7,2,256]{6,5,4,3,2,1,0:T(2,128)(2,1)} fusion(f32[256]{0:T(256)S(1)} %bitcast.117, f32[256]{0:T(256)S(1)} %bitcast.109, f32[4,4,2,7,7,2]{5,4,3,2,1,0:T(8,128)S(1)} %add_rsqrt_fusion, f32[4,4,2,7,7,2]{5,4,3,2,1,0:T(8,128)S(1)} %broadcast_multiply_fusion.2, f32[4,7,4,7,2,2,256]{6,5,4,3,2,1,0:T(2,128)} %reshape.279), kind=kLoop, calls=%fused_computation.42 | loop fusion | flops 4014080 | bytes 4844032 | tf_op jit(solution)/shard_map/convert_element_type | solution.py:27
  95.7 7.4 %copy.53 = bf16[3136,768]{0,1:T(8,128)(2,1)} copy(bf16[3136,768]{1,0:T(8,128)(2,1)} %add_convert_fusion) | data formatting | bytes 9633792 | tf_op jit(solution)/shard_map/convert_element_type | solution.py:96
  103.1 26.4 %reshape.266 = bf16[32,98,3,8,32]{1,0,4,3,2:T(8,128)(2,1)} reshape(bf16[3136,768]{0,1:T(8,128)(2,1)} %copy.53) | data formatting | bytes 9633792 | tf_op jit(solution)/shard_map/reshape | solution.py:99
  129.5 6.5 %fusion.70 = (bf16[32,98,1,8,32]{1,0,4,3,2:T(8,128)(2,1)}, bf16[32,98,1,8,32]{1,0,4,3,2:T(8,128)(2,1)}, bf16[32,98,1,8,32]{1,0,4,3,2:T(8,128)(2,1)S(1)}) fusion(bf16[32,98,3,8,32]{1,0,4,3,2:T(8,128)(2,1)} %reshape.266), kind=kLoop, calls=%fused_computation.136 | loop fusion | bytes 9633792 | tf_op jit(solution)/shard_map/slice | solution.py:101
  136.0 12.9 %fusion.73 = (f32[32,8,98]{2,1,0:T(8,128)}, f32[32,8,98,98]{2,3,1,0:T(8,128)}) fusion(f32[8,98,98]{1,2,0:T(8,128)S(1)} %copy-done.22, pred[32,98,98]{1,2,0:T(8,128)(4,1)S(1)} %copy-done.21, bf16[32,98,1,8,32]{1,0,4,3,2:T(8,128)(2,1)} %get-tuple-element.31, bf16[32,98,1,8,32]{1,0,4,3,2:T(8,128)(2,1)} %get-tuple-element.30), kind=kOutput, calls=%fused_computation.139 | convolution fusion | flops 169645152 | bytes 13760768 | tf_op jit(solution)/shard_map/sub | solution.py:113
  149.0 7.7 %convert_bitcast_fusion.3 = bf16[32,98,8,32]{1,3,2,0:T(8,128)(2,1)S(1)} fusion(bf16[32,98,1,8,32]{1,0,4,3,2:T(8,128)(2,1)S(1)} %get-tuple-element.32, f32[32,8,98,98]{2,3,1,0:T(8,128)} %get-tuple-element.38, f32[32,8,98]{2,1,0:T(8,128)} %get-tuple-element.37), kind=kOutput, calls=%fused_computation.65 | convolution fusion | flops 163072000 | bytes 13146112 | tf_op jit(solution)/shard_map/bhqk,bkhd->bqhd/dot_general | solution.py:116
  167.9 8.0 %multiply_convert_fusion.1 = (bf16[3136,1024]{1,0:T(8,128)(2,1)S(1)}, f32[3136,1024]{1,0:T(8,128)}) fusion(bf16[256,1024]{1,0:T(8,128)(2,1)S(1)} %copy-done, f32[3136,256]{1,0:T(8,128)S(1)} %get-tuple-element.40, f32[256]{0:T(256)S(1)} %bitcast.123, f32[256]{0:T(256)S(1)} %bitcast.113, f32[3136]{0:T(1024)S(1)} %add_rsqrt_fusion.1, ...), kind=kOutput, calls=%fused_computation.20 | convolution fusion | flops 1677082624 | bytes 23030272 | tf_op jit(solution)/shard_map/dot_general | solution.py:122
  175.9 11.2 %fusion.13 = bf16[3136,1024]{1,0:T(8,128)(2,1)S(1)} fusion(f32[3136,1024]{1,0:T(8,128)} %get-tuple-element.42, bf16[3136,256]{1,0:T(8,128)(2,1)S(1)} %copy-done.7, bf16[1024,256]{1,0:T(8,128)(2,1)S(1)} %copy-done.32), kind=kOutput, calls=%fused_computation.19 | convolution fusion | flops 1708392448 | bytes 21397504 | tf_op jit(solution)/shard_map/dot_general | solution.py:157
  229.3 9.4 %reshape.269 = bf16[32,98,8,32]{1,0,3,2:T(8,128)(2,1)S(1)} reshape(bf16[3136,256]{0,1:T(8,128)(2,1)} %copy.62) | data formatting | bytes 3211264 | tf_op jit(solution)/shard_map/reshape | solution.py:182
  238.8 10.0 %convert_bitcast_fusion = bf16[32,98,1,8,32]{1,4,3,0,2:T(8,128)(2,1)} fusion(bf16[32,98,8,32]{1,0,3,2:T(8,128)(2,1)S(1)} %reshape.269, f32[32,8,98,98]{2,3,1,0:T(8,128)} %get-tuple-element.38, f32[32,8,98]{2,1,0:T(8,128)S(1)} %copy-done.36), kind=kOutput, calls=%fused_computation.62 | convolution fusion | flops 163072000 | bytes 13146112 | tf_op jit(solution)/shard_map/bhqk,bqhd->bkhd/dot_general | solution.py:186
  248.8 7.7 %fusion.35 = f32[32,8,98,98]{2,3,1,0:T(8,128)} fusion(bf16[32,98,1,8,32]{1,0,4,3,2:T(8,128)(2,1)S(1)} %copy-done.10, bf16[32,98,8,32]{1,0,3,2:T(8,128)(2,1)S(1)} %reshape.269), kind=kOutput, calls=%fused_computation.67 | convolution fusion | flops 157351936 | bytes 13045760 | tf_op jit(solution)/shard_map/bqhd,bkhd->bhqk/dot_general | solution.py:183
  256.4 23.2 %convert_bitcast_fusion.1 = bf16[32,98,1,8,32]{1,4,3,0,2:T(8,128)(2,1)} fusion(bf16[32,98,1,8,32]{1,0,4,3,2:T(8,128)(2,1)} %get-tuple-element.31, f32[32,8,98,98]{2,3,1,0:T(8,128)} %fusion.35, f32[32,8,98,98]{2,3,1,0:T(8,128)} %get-tuple-element.38, f32[32,8,98]{2,1,0:T(8,128)S(1)} %copy-done.36), kind=kOutput, calls=%fused_computation.63 | convolution fusion | flops 175390304 | bytes 22980608 | tf_op jit(solution)/shard_map/bhqk,bqhd->bkhd/dot_general | solution.py:196
  279.6 23.3 %convert_bitcast_fusion.2 = bf16[32,98,1,8,32]{1,4,3,0,2:T(8,128)(2,1)} fusion(bf16[32,98,1,8,32]{1,0,4,3,2:T(8,128)(2,1)S(1)} %copy-done.15, f32[32,8,98,98]{2,3,1,0:T(8,128)} %fusion.35, f32[32,8,98,98]{2,3,1,0:T(8,128)} %get-tuple-element.38, f32[32,8,98]{2,1,0:T(8,128)S(1)} %copy-done.36), kind=kOutput, calls=%fused_computation.64 | convolution fusion | flops 175390304 | bytes 22980608 | tf_op jit(solution)/shard_map/bhqk,bkhd->bqhd/dot_general | solution.py:193
  302.9 20.6 %fusion.75 = f32[8,98,98]{1,2,0:T(8,128)S(1)} fusion(f32[32,8,98,98]{2,3,1,0:T(8,128)} %fusion.35, f32[32,8,98,98]{2,3,1,0:T(8,128)} %get-tuple-element.38, f32[32,8,98]{2,1,0:T(8,128)S(1)} %copy-done.36), kind=kOutput, calls=%fused_computation.141 | output fusion | flops 14700097 | bytes 20076672 | tf_op jit(solution)/shard_map/sub | solution.py:189
  326.2 7.5 %convert_reduce_fusion = (f32[3,8,32]{2,1,0:T(8,128)S(1)}, bf16[32,98,3,8,32]{1,4,3,0,2:T(8,128)(2,1)}) fusion(bf16[32,98,1,8,32]{1,4,3,0,2:T(8,128)(2,1)} %convert_bitcast_fusion, bf16[32,98,1,8,32]{1,4,3,0,2:T(8,128)(2,1)} %convert_bitcast_fusion.1, bf16[32,98,1,8,32]{1,4,3,0,2:T(8,128)(2,1)} %convert_bitcast_fusion.2), kind=kLoop, calls=%fused_computation.21 | loop fusion | flops 9633024 | bytes 9636864 | tf_op jit(solution)/shard_map/reduce_sum | solution.py:203
  333.8 9.5 %copy.68 = bf16[32,98,3,8,32]{1,0,4,3,2:T(8,128)(2,1)} copy(bf16[32,98,3,8,32]{1,4,3,0,2:T(8,128)(2,1)} %get-tuple-element.29) | data formatting | bytes 9633792 | tf_op jit(solution)/shard_map/stack | solution.py:199
  343.3 13.0 %reshape.270 = bf16[3136,768]{0,1:T(8,128)(2,1)} reshape(bf16[32,98,3,8,32]{1,0,4,3,2:T(8,128)(2,1)} %copy.68) | data formatting | bytes 9633792 | tf_op jit(solution)/shard_map/reshape | solution.py:199
  356.3 8.5 %multiply_reduce_fusion.2 = (f32[256]{0:T(256)S(1)}, f32[3136]{0:T(1024)S(1)}, f32[3136]{0:T(1024)S(1)}, f32[256]{0:T(256)S(1)}, f32[3136,256]{1,0:T(8,128)}) fusion(f32[3136,256]{1,0:T(8,128)} %reshape.272, f32[3136]{0:T(1024)S(1)} %copy-done.26, f32[3136]{0:T(1024)S(1)} %copy-done.24, f32[256]{0:T(256)S(1)} %bitcast.111, bf16[3136,768]{0,1:T(8,128)(2,1)} %reshape.270, ...), kind=kOutput, calls=%fused_computation.44 | convolution fusion | flops 1240344064 | bytes 11685888 | tf_op jit(solution)/shard_map/dot_general | solution.py:204
  367.3 6.7 %add_convert_fusion.2 = bf16[3136,256]{1,0:T(8,128)(2,1)} fusion(f32[3136,256]{1,0:T(8,128)} %copy-done.3, f32[3136,256]{1,0:T(8,128)} %get-tuple-element.44, f32[3136,256]{1,0:T(8,128)} %reshape.272, f32[3136]{0:T(1024)S(1)} %broadcast_multiply_fusion.6, f32[3136]{0:T(1024)S(1)} %broadcast_multiply_fusion.7, f32[256]{0:T(256)S(1)} %bitcast.112, ...), kind=kLoop, calls=%fused_computation.45 | loop fusion | flops 7225344 | bytes 11290624 | tf_op jit(solution)/shard_map/convert_element_type | solution.py:207
  385.1 6.1 %fusion.2 = f32[8,507]{1,0:T(8,128)S(1)} fusion(f32[8,9604]{1,0:T(8,128)S(1)} %reshape.271, s32[9604]{0:T(1024)S(1)} %copy-done.28), kind=kOutput, calls=%fused_computation.3 | convolution fusion | flops 472315136 | bytes 361968 | tf_op jit(solution)/shard_map/dot_general | solution.py:191
  391.2 64.6 %all-reduce = (f32[1,256]{1,0:T(1,128)S(1)}, f32[1,256]{1,0:T(1,128)S(1)}, f32[1,256]{1,0:T(1,128)S(1)}, f32[1,256]{1,0:T(1,128)S(1)}, f32[768]{0:T(1024)S(1)}, /*index=5*/f32[8,507]{1,0:T(8,128)S(1)}) all-reduce(f32[1,256]{1,0:T(1,128)S(1)} %bitcast.119, ...), channel_id=1, replica_groups=mesh['lat'=8,'lon'=16] {'lat','lon'}, use_global_device_ids=true, to_apply=%region_14.15 | all-reduce | flops 5848 | bytes 46784 | tf_op jit(solution)/shard_map/psum | solution.py:247
  466.7 69.5 %all-reduce.4.cloned.1.call-done = (f32[256,768]{1,0:T(8,128)}, f32[256,256]{1,0:T(8,128)}, f32[256,1024]{1,0:T(8,128)}, f32[1024,256]{1,0:T(8,128)}) async-done(((f32[256,768]{1,0:T(8,128)}, f32[256,256]{1,0:T(8,128)}, f32[256,1024]{1,0:T(8,128)}, f32[1024,256]{1,0:T(8,128)}), (f32[256,768]{1,0:T(8,128)}, f32[256,256]{1,0:T(8,128)}, f32[256,1024]{1,0:T(8,128)}, ...) | async-done | bytes 3145744 | tf_op jit(solution)/shard_map/psum | solution.py:247
  (172 shorter events, 152.4 us)
Async XLA Ops:
  7.2 160.7 %copy-start = (bf16[256,1024]{1,0:T(8,128)(2,1)S(1)}, bf16[256,1024]{1,0:T(8,128)(2,1)}, u32[]{:S(2)}) copy-start(bf16[256,1024]{1,0:T(8,128)(2,1)} %param.17) | copy-start | bytes 1572868
  7.2 529.0 %all-reduce.4.cloned.1.call-start = ((), (), s32[]{:S(2)}) async-start(), calls=%async_computation | async-start | bytes 6291456 | tf_op jit(solution)/shard_map/psum | solution.py:247
  8.9 30.6 %collective-permute-start.4 = (bf16[1,28,3,4,256]{4,3,2,1,0:T(4,128)(2,1)}, bf16[1,28,3,4,256]{4,3,2,1,0:T(4,128)(2,1)}, u32[]{:S(2)}, u32[]{:S(2)}) collective-permute-start(bf16[1,28,3,4,256]{4,3,2,1,0:T(4,128)(2,1)} %slice.104), channel_id=1, source_target_pairs={{0,15},{1,0},{2,1},{3,2},{4,3},{5,4},{6,5},{7,6},{8,7},{9,8},{10,9... | collective-permute-start | bytes 516104 | tf_op jit(solution)/shard_map/ppermute | solution.py:19
  12.0 23.4 %collective-permute-start = (bf16[1,28,3,4,256]{4,3,2,1,0:T(4,128)(2,1)}, bf16[1,28,3,4,256]{4,3,2,1,0:T(4,128)(2,1)}, u32[]{:S(2)}, u32[]{:S(2)}) collective-permute-start(bf16[1,28,3,4,256]{4,3,2,1,0:T(4,128)(2,1)} %slice.95), channel_id=1, source_target_pairs={{0,15},{1,0},{2,1},{3,2},{4,3},{5,4},{6,5},{7,6},{8,7},{9,8},{10,9... | collective-permute-start | bytes 516104 | tf_op jit(solution)/shard_map/ppermute | solution.py:19
  18.4 72.9 %copy-start.29 = (f32[1,256]{1,0:T(1,128)}, f32[1,256]{1,0:T(1,128)S(1)}, u32[]{:S(2)}) copy-start(f32[1,256]{1,0:T(1,128)S(1)} %get-tuple-element.34) | copy-start | bytes 3076
  36.3 10.5 %collective-permute-start.1 = (bf16[1,3,28,4,256]{4,3,2,1,0:T(4,128)(2,1)S(1)}, bf16[1,3,28,4,256]{4,3,2,1,0:T(4,128)(2,1)S(1)}, u32[]{:S(2)}, u32[]{:S(2)}) collective-permute-start(bf16[1,3,28,4,256]{4,3,2,1,0:T(4,128)(2,1)S(1)} %pad_maximum_fusion.7), channel_id=1, source_target_pairs={{0,112},{16,0},{32,16},{48,32},{64,48},{80,64},{96,80},{112,96},{1... | collective-permute-start | bytes 516104 | tf_op jit(solution)/shard_map/ppermute | solution.py:19
  41.1 27.8 %collective-permute-start.5 = (bf16[1,3,28,4,256]{4,3,2,1,0:T(4,128)(2,1)}, bf16[1,3,28,4,256]{4,3,2,1,0:T(4,128)(2,1)}, u32[]{:S(2)}, u32[]{:S(2)}) collective-permute-start(bf16[1,3,28,4,256]{4,3,2,1,0:T(4,128)(2,1)} %pad_maximum_fusion.5), channel_id=1, source_target_pairs={{0,112},{16,0},{32,16},{48,32},{64,48},{80,64},{96,80},{112,96},{1... | collective-permute-start | bytes 516104 | tf_op jit(solution)/shard_map/ppermute | solution.py:19
  64.0 27.3 %copy-start.23 = (f32[3136]{0:T(1024)}, f32[3136]{0:T(1024)S(1)}, u32[]{:S(2)}) copy-start(f32[3136]{0:T(1024)S(1)} %div.57) | copy-start | bytes 37636
  78.1 13.1 %copy-start.25 = (f32[3136]{0:T(1024)}, f32[3136]{0:T(1024)S(1)}, u32[]{:S(2)}) copy-start(f32[3136]{0:T(1024)S(1)} %rsqrt.21) | copy-start | bytes 37636
  136.0 13.0 %copy-start.9 = (bf16[32,98,1,8,32]{1,0,4,3,2:T(8,128)(2,1)}, bf16[32,98,1,8,32]{1,0,4,3,2:T(8,128)(2,1)S(1)}, u32[]{:S(2)}) copy-start(bf16[32,98,1,8,32]{1,0,4,3,2:T(8,128)(2,1)S(1)} %get-tuple-element.32) | copy-start | bytes 4816900
  166.9 29.4 %copy-start.5 = (f32[3136,256]{1,0:T(8,128)}, f32[3136,256]{1,0:T(8,128)S(1)}, u32[]{:S(2)}) copy-start(f32[3136,256]{1,0:T(8,128)S(1)} %get-tuple-element.40) | copy-start | bytes 9633796
  226.8 11.9 %copy-start.36 = (f32[32,8,98]{2,1,0:T(8,128)S(1)}, f32[32,8,98]{2,1,0:T(8,128)}, u32[]{:S(2)}) copy-start(f32[32,8,98]{2,1,0:T(8,128)} %get-tuple-element.37) | copy-start | bytes 301060
  256.4 23.2 %copy-start.15 = (bf16[32,98,1,8,32]{1,0,4,3,2:T(8,128)(2,1)S(1)}, bf16[32,98,1,8,32]{1,0,4,3,2:T(8,128)(2,1)}, u32[]{:S(2)}) copy-start(bf16[32,98,1,8,32]{1,0,4,3,2:T(8,128)(2,1)} %get-tuple-element.30) | copy-start | bytes 4816900
  302.9 20.6 %copy-start.11 = (bf16[4,4,2,7,7,2,256]{6,5,4,3,2,1,0:T(2,128)(2,1)S(1)}, bf16[4,4,2,7,7,2,256]{6,5,4,3,2,1,0:T(2,128)(2,1)}, u32[]{:S(2)}) copy-start(bf16[4,4,2,7,7,2,256]{6,5,4,3,2,1,0:T(2,128)(2,1)} %add_convert_fusion.1) | copy-start | bytes 4816900
  325.0 132.6 %collective-permute-start.2 = (bf16[1,3,28,4,256]{4,3,2,1,0:T(4,128)(2,1)S(1)}, bf16[1,3,28,4,256]{4,3,2,1,0:T(4,128)(2,1)S(1)}, u32[]{:S(2)}, u32[]{:S(2)}) collective-permute-start(bf16[1,3,28,4,256]{4,3,2,1,0:T(4,128)(2,1)S(1)} %slice.101), channel_id=1, source_target_pairs={{0,16},{16,32},{32,48},{48,64},{64,80},{80,96},{96,112},{112,0},{1... | collective-permute-start | bytes 516104 | tf_op jit(solution)/shard_map/ppermute | solution.py:19
  343.3 13.0 %copy-start.24 = (f32[3136]{0:T(1024)S(1)}, f32[3136]{0:T(1024)}, u32[]{:S(2)}) copy-start(f32[3136]{0:T(1024)} %copy-done.23) | copy-start | bytes 37636
  343.3 13.0 %copy-start.26 = (f32[3136]{0:T(1024)S(1)}, f32[3136]{0:T(1024)}, u32[]{:S(2)}) copy-start(f32[3136]{0:T(1024)} %copy-done.25) | copy-start | bytes 37636
  343.3 13.0 %copy-start.30 = (f32[1,256]{1,0:T(1,128)S(1)}, f32[1,256]{1,0:T(1,128)}, u32[]{:S(2)}) copy-start(f32[1,256]{1,0:T(1,128)} %copy-done.29) | copy-start | bytes 3076
  343.3 13.0 %copy-start.34 = (bf16[256,768]{1,0:T(8,128)(2,1)S(1)}, bf16[256,768]{1,0:T(8,128)(2,1)}, u32[]{:S(2)}) copy-start(bf16[256,768]{1,0:T(8,128)(2,1)} %param.14) | copy-start | bytes 1179652
  384.0 77.6 %collective-permute-start.6 = (bf16[1,3,28,4,256]{4,3,2,1,0:T(4,128)(2,1)S(1)}, bf16[1,3,28,4,256]{4,3,2,1,0:T(4,128)(2,1)S(1)}, u32[]{:S(2)}, u32[]{:S(2)}) collective-permute-start(bf16[1,3,28,4,256]{4,3,2,1,0:T(4,128)(2,1)S(1)} %slice.107), channel_id=1, source_target_pairs={{0,16},{16,32},{32,48},{48,64},{64,80},{80,96},{96,112},{112,0},{1... | collective-permute-start | bytes 516104 | tf_op jit(solution)/shard_map/ppermute | solution.py:19
  385.1 72.5 %copy-start.8 = (bf16[1,25,28,4,256]{4,3,2,1,0:T(4,128)(2,1)S(1)}, bf16[1,25,28,4,256]{4,3,2,1,0:T(4,128)(2,1)}, u32[]{:S(2)}) copy-start(bf16[1,25,28,4,256]{4,3,2,1,0:T(4,128)(2,1)} %slice.102) | copy-start | bytes 4300804
  457.7 4.3 collective-permute-start.3
  461.7 2.7 collective-permute-start.7
  464.4 79.1 %copy-start.1 = (bf16[256,1024]{1,0:T(8,128)(2,1)S(1)}, bf16[256,1024]{1,0:T(8,128)(2,1)}, u32[]{:S(2)}) copy-start(bf16[256,1024]{1,0:T(8,128)(2,1)} %param.17) | copy-start | bytes 1572868
  (22 other events, 157.0 us)
Sparse Core Ops, SparseCore 0:
  385.2 150.9 all-reduce.3
where the time goes:
time: 560 us; the launch traced here: 551 us
  matrix products  156 us (28%)
  local copies, waits for them, and re-layouts  145 us (26%)
  other arithmetic  86.2 us (15%)
  waiting for transfers between devices  69.6 us (12%)
  blocking collectives  64.6 us (12%)
  between operations  15 us (3%)
  starting transfers between devices  13.8 us (2%)
    psum x1, waiting for transfers between devices, local(): lax.psum((grad_w_in, grad_w_out, grad_gain2, grad_shift2, grad_w_qkv, gra...  69.5 us
    psum x1, blocking collectives, local(): lax.psum((grad_w_in, grad_w_out, grad_gain2, grad_shift2, grad_w_qkv, gra...  64.6 us
    reshape x1, local copies, waits for them, and re-layouts, forward(): projected = projected.reshape(count, width_tok, 3, heads, head_dim)  26.4 us
    dot_general x1, matrix products, attention_backward(): jnp.einsum('bhqk,bkhd->bqhd', grad_scaled, keys_in, preferred_element_typ...  23.3 us
    dot_general x1, matrix products, attention_backward(): jnp.einsum('bhqk,bqhd->bkhd', grad_scaled, queries, preferred_element_typ...  23.2 us
    sub x1, other arithmetic, attention_backward(): grad_attn - jnp.sum(grad_attn * attention, -1, keepdims=True)  20.6 us
    convert_element_type x3, local copies, waits for them, and re-layouts, forward(): flat = windows.reshape(count * width_tok, channels).astype(jnp.float32)  15.7 us
    ppermute x8, starting transfers between devices, shifted(): return lax.ppermute(value, axis, pairs)  13.8 us
  transfers between devices with their start and end apart: 9, of which 2 were waited for; matrix products, arithmetic and copies ran while one was open for 22% of the time, Pallas kernels for 0%

commit v1 on v0

v1 whole, which is shorter than its diff:
```python
import functools

import jax
import jax.numpy as jnp
import numpy as np
from jax import lax
from jax.experimental import pallas as pl
from jax.experimental.pallas import tpu as pltpu
from jax.sharding import PartitionSpec as P

WIN = 7
LEV = 4
WLEV = 2
SHIFT = 3
EPS = 1e-05
NEG = -1e30
HEADS = 8
HD = 32
C = 256
FF = 1024
SLAB = 16
WROWS = WIN * SLAB
HALF = HEADS // 2
PAIR = 2 * 128
NREL = 507
BF = jnp.bfloat16
F32 = jnp.float32

NN = (((1,), (0,)), ((), ()))
NT = (((1,), (1,)), ((), ()))
TN = (((0,), (0,)), ((), ()))


def dot(a, b, dims=NN):
    return lax.dot_general(a, b, dims, preferred_element_type=F32)


def placement():
    matrix = np.zeros((128, 128), np.float32)
    for wc in range(4):
        for lw in range(2):
            for b in range(WIN):
                for l in range(WLEV):
                    row = (wc * 2 + lw) * SLAB + b * WLEV + l
                    matrix[row, (wc * WIN + SHIFT + b) * LEV + lw * WLEV + l] = 1.0
    return matrix


def strip_map():
    index = np.full((SLAB, 256), -1, np.int32)
    for bk in range(WIN):
        for lk in range(WLEV):
            for da in range(13):
                for bq in range(WIN):
                    for lq in range(WLEV):
                        index[bk * WLEV + lk, da * SLAB + bq * WLEV + lq] = (
                            (da * 13 + bq - bk + 6) * 3 + lq - lk + 1
                        )
    return index


def layer_norm(x, gain, shift):
    center = x - jnp.mean(x, -1, keepdims=True)
    istd = lax.rsqrt(jnp.mean(center * center, -1, keepdims=True) + EPS)
    xhat = center * istd
    return xhat, istd, (xhat * gain + shift).astype(BF)


def norm_backward(up, xhat, istd, gain):
    n = up * gain
    return istd * (n - jnp.mean(n, -1, keepdims=True) - xhat * jnp.mean(n * xhat, -1, keepdims=True))


def gelu_both(p):
    c0 = np.float32(np.sqrt(2.0 / np.pi))
    c1 = np.float32(0.044715 * np.sqrt(2.0 / np.pi))
    p2 = p * p
    t = jnp.tanh(p * (c0 + c1 * p2))
    h = 0.5 * p
    half = 0.5 + 0.5 * t
    act = p * half
    slope = half + h * (1.0 - t * t) * (c0 + (3.0 * c1) * p2)
    return act, slope


def head_masks():
    lane = lax.broadcasted_iota(jnp.int32, (1, C), 1) // HD
    pair = [((lane % HALF) == j) for j in range(HALF)]
    group = [((lane // HALF) == g) for g in range(2)]
    return pair, group


def stack_pairs(v, pair):
    return jnp.concatenate([v * m.astype(BF) for m in pair], 0)


def stack_groups(v, group):
    pad = jnp.zeros((128 - WROWS, C), BF)
    return jnp.concatenate([v * group[0].astype(BF), pad, v * group[1].astype(BF), pad], 0)


def pick_pairs(r, pair):
    out = r[3 * WROWS:4 * WROWS]
    for j in range(3):
        out = jnp.where(pair[j], r[j * WROWS:(j + 1) * WROWS], out)
    return out


def down_keys(vt, low):
    parts = [None] * HEADS
    for j in range(HALF):
        lhs = jnp.concatenate([vt[j * HD:(j + 1) * HD], vt[(j + HALF) * HD:(j + HALF + 1) * HD]], 0)
        out = dot(lhs, low[j * WROWS:(j + 1) * WROWS])
        parts[j] = out[:HD, :128]
        parts[j + HALF] = out[HD:, 128:]
    return jnp.concatenate(parts, 0).T[:WROWS]


def compute(refs, s, chunk_windows=4):
    pair, group = head_masks()
    scale = np.float32(HD ** -0.5)
    CH = chunk_windows * WROWS
    nwin = 32

    def gather(src, dst):
        def row(r, _):
            y = dot(s.pm[...], src[r]).astype(BF)
            wr, a = r // WIN, r % WIN
            for c in range(8):
                dst[pl.ds(pl.multiple_of((wr * 8 + c) * WROWS + a * SLAB, SLAB), SLAB), :] = y[c * SLAB:(c + 1) * SLAB]
            return 0
        lax.fori_loop(0, 28, row, 0, unroll=2)

    gather(s.x, s.z)
    gather(s.g, s.gz)

    key_row = lax.broadcasted_iota(jnp.int32, (WROWS, 256), 0)
    lane = lax.broadcasted_iota(jnp.int32, (WROWS, 256), 1)
    qa, ka = (lane % 128) // SLAB, key_row // SLAB
    empty = (key_row % SLAB) >= WIN * WLEV
    cut = jnp.logical_and((qa >= WIN - SHIFT) != (ka >= WIN - SHIFT), s.last)
    for j in range(HALF):
        tiles = []
        for g in range(2):
            strip = s.strip[j + HALF * g]
            rows = [strip[:, (6 - ak) * SLAB:(6 - ak) * SLAB + WROWS] for ak in range(WIN)]
            tile = jnp.concatenate(rows, 0)
            tiles.append(jnp.concatenate([tile, jnp.zeros((WROWS, 128 - WROWS), F32)], 1))
        full = jnp.where(empty, NEG, jnp.concatenate(tiles, 1))
        s.bias[0, j * WROWS:(j + 1) * WROWS] = full
        s.bias[1, j * WROWS:(j + 1) * WROWS] = jnp.where(cut, NEG, full)
    s.dbias[...] = jnp.zeros_like(s.dbias)
    s.gw_in[...] = jnp.zeros_like(s.gw_in)
    s.gw_out[...] = jnp.zeros_like(s.gw_out)
    s.gw_qkv[...] = jnp.zeros_like(s.gw_qkv)
    s.gw_proj[...] = jnp.zeros_like(s.gw_proj)
    s.small[...] = jnp.zeros_like(s.small)

    def forward_window(w):
        rows = pl.ds(pl.multiple_of(w * WROWS, WROWS), WROWS)
        arows = pl.multiple_of(w * (HALF * WROWS), HALF * WROWS)
        q, k, v = s.p[rows, 0:C], s.p[rows, C:2 * C], s.p[rows, 2 * C:3 * C]
        scores = dot(stack_pairs(k, pair), stack_groups(q, group), NT)
        which = (w >= 24).astype(jnp.int32)
        vt = v.T
        lows = []
        for j in range(HALF):
            t = scores[j * WROWS:(j + 1) * WROWS] * scale + s.bias[which, j * WROWS:(j + 1) * WROWS]
            e = jnp.exp(t - jnp.max(t, 0, keepdims=True))
            att = e * (1.0 / jnp.sum(e, 0, keepdims=True))
            s.att[pl.ds(arows + j * WROWS, WROWS), :] = att
            lows.append(att.astype(BF))
        s.mixed[rows, :] = down_keys(vt, jnp.concatenate(lows, 0)).astype(BF)

    def phase_a(i, _):
        rows = pl.ds(pl.multiple_of(i * CH, CH), CH)
        x = s.z[rows, :].astype(F32)
        _, _, hidden1 = layer_norm(x, s.gains[0:1], s.shifts[0:1])
        s.p[rows, :] = (dot(hidden1, s.w_qkv[...]) + s.b_qkv[...]).astype(BF)

        def win(w, _):
            forward_window(i * chunk_windows + 2 * w)
            forward_window(i * chunk_windows + 2 * w + 1)
            return 0
        lax.fori_loop(0, chunk_windows // 2, win, 0)

        mixed = s.mixed[rows, :]
        resid = s.z[rows, :].astype(F32) + dot(mixed, s.w_proj[...])
        xhat2, istd2, hidden2 = layer_norm(resid, s.gains[1:2], s.shifts[1:2])
        act, slope = gelu_both(dot(hidden2, s.w_in[...]))
        act = act.astype(BF)
        s.out[rows, :] = (resid + dot(act, s.w_out[...])).astype(BF)
        gr = s.gz[rows, :]
        s.gw_out[...] += dot(gr, act, TN)
        gp = (dot(gr, s.w_out[...], NT) * slope).astype(BF)
        s.gw_in[...] += dot(hidden2, gp, TN)
        gh = dot(gp, s.w_in[...], NT)
        s.small[1:2, 0:C] += jnp.sum(gh * xhat2, 0, keepdims=True)
        s.small[3:4, 0:C] += jnp.sum(gh, 0, keepdims=True)
        gres = gr.astype(F32) + norm_backward(gh, xhat2, istd2, s.gains[1:2])
        s.gres[rows, :] = gres
        low = gres.astype(BF)
        s.gw_proj[...] += dot(mixed, low, TN)
        s.gm[rows, :] = dot(low, s.w_proj[...], NT).astype(BF)
        return 0

    lax.fori_loop(0, nwin // chunk_windows, phase_a, 0)

    def backward_window(w):
        rows = pl.ds(pl.multiple_of(w * WROWS, WROWS), WROWS)
        arows = pl.multiple_of(w * (HALF * WROWS), HALF * WROWS)
        q, k, v = s.p[rows, 0:C], s.p[rows, C:2 * C], s.p[rows, 2 * C:3 * C]
        gm2 = stack_groups(s.gm[rows, :], group)
        ga = dot(stack_pairs(v, pair), gm2, NT)
        lows, dlows = [], []
        for j in range(HALF):
            att = s.att[pl.ds(arows + j * WROWS, WROWS), :]
            t = att * ga[j * WROWS:(j + 1) * WROWS]
            ds = t - att * jnp.sum(t, 0, keepdims=True)
            s.dbias[j * WROWS:(j + 1) * WROWS] += ds
            lows.append(att.astype(BF))
            dlows.append((ds * scale).astype(BF))
        low, dlow = jnp.concatenate(lows, 0), jnp.concatenate(dlows, 0)
        gv = pick_pairs(dot(low, gm2), pair).astype(BF)
        gk = pick_pairs(dot(dlow, stack_groups(q, group)), pair).astype(BF)
        gq = down_keys(k.T, dlow).astype(BF)
        s.p[rows, 0:C] = gq
        s.p[rows, C:2 * C] = gk
        s.p[rows, 2 * C:3 * C] = gv

    def phase_b(i, _):
        rows = pl.ds(pl.multiple_of(i * CH, CH), CH)

        def win(w, _):
            backward_window(i * chunk_windows + 2 * w)
            backward_window(i * chunk_windows + 2 * w + 1)
            return 0
        lax.fori_loop(0, chunk_windows // 2, win, 0)
        xhat, istd, hidden = layer_norm(s.z[rows, :].astype(F32), s.gains[0:1], s.shifts[0:1])
        gp = s.p[rows, :]
        s.gw_qkv[...] += dot(hidden, gp, TN)
        s.small[4:5, :] += jnp.sum(gp.astype(F32), 0, keepdims=True)
        gh = dot(gp, s.w_qkv[...], NT)
        s.small[0:1, 0:C] += jnp.sum(gh * xhat, 0, keepdims=True)
        s.small[2:3, 0:C] += jnp.sum(gh, 0, keepdims=True)
        s.gout[rows, :] = (s.gres[rows, :] + norm_backward(gh, xhat, istd, s.gains[0:1])).astype(BF)
        return 0

    lax.fori_loop(0, nwin // chunk_windows, phase_b, 0)

    for h in range(HEADS):
        j, g = h % HALF, h // HALF
        total = None
        for ak in range(WIN):
            piece = s.dbias[j * WROWS + ak * SLAB:j * WROWS + (ak + 1) * SLAB, g * 128:g * 128 + WROWS]
            before = (6 - ak) * SLAB
            parts = []
            if before:
                parts.append(jnp.zeros((SLAB, before), F32))
            parts.append(piece)
            parts.append(jnp.zeros((SLAB, 256 - before - WROWS), F32))
            moved = jnp.concatenate(parts, 1)
            total = moved if total is None else total + moved
        s.dstrip[h] = total

    def scatter(src, dst):
        def row(r, _):
            wr, a = r // WIN, r % WIN
            y = jnp.concatenate(
                [src[pl.ds(pl.multiple_of((wr * 8 + c) * WROWS + a * SLAB, SLAB), SLAB), :] for c in range(8)], 0
            )
            dst[r] = dot(s.pm[...], y, TN).astype(BF)
            return 0
        lax.fori_loop(0, 28, row, 0, unroll=2)

    scatter(s.out, s.res)
    scatter(s.gout, s.ing)


class Refs:
    pass


INS = ("x", "g", "pm", "strip", "gains", "shifts", "w_qkv", "b_qkv", "w_proj", "w_in", "w_out")
OUTS = ("res", "ing", "gw_in", "gw_out", "gw_qkv", "gw_proj", "small", "dstrip")
SCR = ("z", "gz", "p", "att", "mixed", "out", "gout", "gres", "gm", "bias", "dbias")


def kernel(*refs):
    s = Refs()
    for name, ref in zip(INS + OUTS + SCR, refs):
        setattr(s, name, ref)
    s.last = lax.axis_index("lat") == lax.axis_size("lat") - 1
    compute(refs, s)


def fused(x, g, pm, strip, gains, shifts, w_qkv, b_qkv, w_proj, w_in, w_out):
    T = 32 * WROWS
    sds = jax.ShapeDtypeStruct
    vm = pl.BlockSpec(memory_space=pltpu.VMEM)
    return pl.pallas_call(
        kernel,
        out_shape=(
            sds((28, 128, C), BF), sds((28, 128, C), BF), sds((C, FF), F32), sds((C, FF), F32),
            sds((C, 3 * C), F32), sds((C, C), F32), sds((8, 3 * C), F32), sds((HEADS, SLAB, 256), F32),
        ),
        in_specs=[vm] * len(INS),
        out_specs=[vm] * len(OUTS),
        scratch_shapes=[
            pltpu.VMEM((T, C), BF), pltpu.VMEM((T, C), BF), pltpu.VMEM((T, 3 * C), BF),
            pltpu.VMEM((T * HALF, 256), F32), pltpu.VMEM((T, C), BF), pltpu.VMEM((T, C), BF),
            pltpu.VMEM((T, C), BF), pltpu.VMEM((T, C), F32), pltpu.VMEM((T, C), BF),
            pltpu.VMEM((2, HALF * WROWS, 256), F32), pltpu.VMEM((HALF * WROWS, 256), F32),
        ],
        compiler_params=pltpu.CompilerParams(vmem_limit_bytes=60 * 1024 * 1024),
        name="windows",
    )(x, g, pm, strip, gains, shifts, w_qkv, b_qkv, w_proj, w_in, w_out)


def shifted(value, axis, steps):
    count = lax.axis_size(axis)
    return lax.ppermute(value, axis, [(i, (i + steps) % count) for i in range(count)])


def roll_in(block):
    wide = jnp.concatenate([block, shifted(block[:, :16], "lon", -1)], 1)
    return jnp.concatenate([wide[SHIFT:], shifted(wide[:SHIFT], "lat", -1)], 0)


def roll_out(block):
    tall = jnp.concatenate([shifted(block[-SHIFT:], "lat", 1), block[:-SHIFT]], 0)
    got = shifted(tall[:, 112:], "lon", 1)
    return jnp.concatenate([tall[:, :16] + got, tall[:, 16:112]], 1)


def local(tokens, out_grad, gains, shifts, w_qkv, b_qkv, w_proj, w_in, w_out, rel_bias):
    rows_n, cols_n, levels, channels = tokens.shape
    total = rows_n * lax.axis_size("lat") * cols_n * lax.axis_size("lon") * levels
    x = roll_in(tokens.reshape(rows_n, cols_n * levels, channels))
    g = roll_in(out_grad.reshape(rows_n, cols_n * levels, channels))
    index = jnp.asarray(strip_map().reshape(-1))
    onehot = (index[:, None] == jnp.arange(NREL, dtype=jnp.int32)[None, :]).astype(F32)
    strip = lax.dot_general(rel_bias, onehot, NT, precision=lax.Precision.HIGHEST).reshape(HEADS, SLAB, 256)
    pm = jnp.asarray(placement(), BF)
    res, ing, gw_in, gw_out, gw_qkv, gw_proj, small, dstrip = fused(
        x, g, pm, strip, gains, shifts, w_qkv, b_qkv[None], w_proj, w_in, w_out
    )
    table = lax.dot_general(dstrip.reshape(HEADS, -1), onehot, NN, precision=lax.Precision.HIGHEST)
    sums = lax.psum((gw_in, gw_out, gw_qkv, gw_proj, small, table), ("lat", "lon"))
    gw_in, gw_out, gw_qkv, gw_proj, small, table = [v * float(total) ** -0.5 for v in sums]
    shape = tokens.shape
    return (
        roll_out(res).reshape(shape), roll_out(ing).reshape(shape),
        small[0:2, :C], small[2:4, :C], gw_qkv, small[4], gw_proj, gw_in, gw_out.T, table,
    )


def solution(mesh):
    big = P("lat", "lon", None, None)
    return jax.shard_map(
        local, mesh=mesh, in_specs=(big, big) + (P(),) * 8, out_specs=(big, big) + (P(),) * 8, check_vma=False
    )
```

time: 560 us -> 366 us (0.65); the launches traced: 551 us -> 365 us
  matrix products: 156 us -> 7.11 us
  local copies, waits for them, and re-layouts: 145 us -> 20.4 us
  Pallas kernels: 0 us -> 84.8 us
  other arithmetic: 86.2 us -> 14.1 us
  waiting for transfers between devices: 69.6 us -> 138 us
    dot_general x19 -> x2, matrix products: 143 us -> 7.11 us  [the longest x1 4.42 us: local(): lax.dot_general(rel_bias, onehot, NT, precision=lax.Precision.HIGHEST)]
    pallas_call x0 -> x1, Pallas kernels: none -> 84.8 us  [fused(): pl.pallas_call(kernel, out_shape=(sds((28, 128, C), BF), sds((28, 128, C)...]
    psum x1, waiting for transfers between devices: 69.5 us -> 132 us  [local(): lax.psum((gw_in, gw_out, gw_qkv, gw_proj, small, table), ('lat', 'lon'))]
    reshape x6 -> x4, local copies, waits for them, and re-layouts: 53.6 us -> 10.8 us  [the longest x1 3.89 us: local(): roll_out(ing).reshape(shape)]
    another operation x8 -> x0, local copies, waits for them, and re-layouts: 32.3 us -> none  [the longest x1 9.49 us: attention_backward(): jnp.stack([grad_queries, grad_keys, grad_values], 2)]
    convert_element_type x7 -> x0, local copies, waits for them, and re-layouts: 29.7 us -> none  [the longest x3 15.7 us: forward(): flat = windows.reshape(count * width_tok, channels).astype(jnp.float32)]
    sub x2 -> x0, other arithmetic: 20.7 us -> none  [the longest x1 20.6 us: attention_backward(): grad_attn - jnp.sum(grad_attn * attention, -1, keepdims=True)]
    reduce_sum x4 -> x0, other arithmetic: 17.1 us -> none  [the longest x1 7.55 us: attention_backward(): grad_b_qkv = jnp.sum(grad_proj, 0, dtype=jnp.float32)]
  transfers between devices with their start and end apart: 9 -> 9, of which waited for: 2 -> 2; matrix products, arithmetic and copies ran while one was open for 22% -> 6% of each run, Pallas kernels for 0% -> 0%
where the time goes in v1:
time: 366 us; the launch traced here: 365 us
  waiting for transfers between devices  138 us (38%)
  Pallas kernels  84.8 us (23%)
  blocking collectives  69.5 us (19%)
  local copies, waits for them, and re-layouts  20.4 us (6%)
  starting transfers between devices  17.2 us (5%)
  between operations  14.3 us (4%)
  other arithmetic  14.1 us (4%)
  matrix products  7.11 us (2%)
    psum x1, waiting for transfers between devices, local(): lax.psum((gw_in, gw_out, gw_qkv, gw_proj, small, table), ('lat', 'lon'))  132 us
    pallas_call x1, Pallas kernels, fused(): pl.pallas_call(kernel, out_shape=(sds((28, 128, C), BF), sds((28, 128, C)...  84.8 us
    psum x1, blocking collectives, local(): lax.psum((gw_in, gw_out, gw_qkv, gw_proj, small, table), ('lat', 'lon'))  69.5 us
    ppermute x8, starting transfers between devices, shifted(): lax.ppermute(value, axis, [(i, (i + steps) % count) for i in range(count)])  17.2 us
  transfers between devices with their start and end apart: 9, of which 2 were waited for; matrix products, arithmetic and copies ran while one was open for 6% of the time, Pallas kernels for 0%

profile of v1, /device:TPU:1, one launch (start us, length us, event | category | flops | bytes accessed | tf_op | source)
XLA Modules:
  0.0 365.0 jit_solution(4835622806372956030)
XLA Ops:
  7.2 2.8 reshape.39
  10.8 1.4 collective-permute-start
  12.2 2.8 reshape.40
  15.0 5.7 %collective-permute-start.2 = (bf16[28,16,256]{2,1,0:T(8,128)(2,1)S(1)}, bf16[28,16,256]{2,1,0:T(8,128)(2,1)S(1)}, u32[]{:S(2)}, u32[]{:S(2)}) collective-permute-start(bf16[28,16,256]{2,1,0:T(8,128)(2,1)S(1)} %slice.79), channel_id=1, source_target_pairs={{0,15},{1,0},{2,1},{3,2},{4,3},{5,4},{6,5},{7,6},{8,7},{9,8},{10,9... | collective-permute-start | bytes 688136 | tf_op jit(solution)/shard_map/ppermute | solution.py:322
  21.1 3.3 collective-permute-start.1
  25.4 4.4 %fusion.1 = f32[4096,8]{0,1:T(8,128)S(1)} fusion(f32[8,507]{1,0:T(8,128)S(1)} %copy-done, s32[4096]{0:T(1024)S(1)} %copy-done.7), kind=kOutput, calls=%fused_computation.2 | convolution fusion | flops 201437184 | bytes 163680 | tf_op jit(solution)/shard_map/dot_general | solution.py:343
  31.4 1.4 pad_maximum_fusion.refs_0_
  32.8 1.4 pad_maximum_fusion.1.refs_1_
  34.2 84.8 %windows.1 = (bf16[28,128,256]{2,1,0:T(8,128)(2,1)}, bf16[28,128,256]{2,1,0:T(8,128)(2,1)}, f32[256,1024]{1,0:T(8,128)}, f32[256,1024]{1,0:T(8,128)}, f32[256,76...) custom-call(bf16[28,128,256]{2,1,0:T(8,128)(2,1)} %pad_maximum_fusion.refs_0_, ...), custom_call_target="tpu_custom_call" | custom-call | tf_op jit(solution)/shard_map/windows/pallas_call | solution.py:301
  119.0 1.7 slice.63
  120.7 1.6 slice.64
  123.4 2.7 fusion
  126.1 69.5 %all-reduce = (f32[8,768]{1,0:T(8,128)S(1)}, f32[8,507]{1,0:T(8,128)S(1)}) all-reduce(f32[8,768]{1,0:T(8,128)S(1)} %copy-done.5, f32[8,507]{1,0:T(8,128)S(1)} %fusion), channel_id=1, replica_groups=mesh['lat'=8,'lon'=16] {'lat','lon'}, use_global_device_ids=true, to_apply=%region_0.0 | all-reduce | flops 10200 | bytes 81600 | tf_op jit(solution)/shard_map/psum | solution.py:349
  195.6 1.5 collective-permute-start.4
  198.4 5.1 %collective-permute-done.6 = bf16[3,128,256]{2,1,0:T(8,128)(2,1)} collective-permute-done((bf16[3,128,256]{2,1,0:T(8,128)(2,1)}, bf16[3,128,256]{2,1,0:T(8,128)(2,1)}, u32[]{:S(2)}, u32[]{:S(2)}) %collective-permute-start.6) | collective-permute-done | bytes 196640 | tf_op jit(solution)/shard_map/ppermute | solution.py:322
  204.2 2.7 collective-permute-start.7
  208.3 1.6 collective-permute-start.5
  210.7 2.2 fusion.11
  212.9 3.9 %reshape.43 = bf16[28,28,4,256]{3,2,1,0:T(4,128)(2,1)} reshape(bf16[28,112,256]{2,1,0:T(8,128)(2,1)} %fusion.11) | data formatting | bytes 3211264 | tf_op jit(solution)/shard_map/reshape | solution.py:353
  218.0 1.4 reshape.42
  219.3 132.5 %all-reduce.4.cloned.1.call-done = (f32[256,768]{1,0:T(8,128)}, f32[256,256]{1,0:T(8,128)}, f32[256,1024]{1,0:T(8,128)}, f32[256,1024]{1,0:T(8,128)}) async-done(((f32[256,768]{1,0:T(8,128)}, f32[256,256]{1,0:T(8,128)}, f32[256,1024]{1,0:T(8,128)}, f32[256,1024]{1,0:T(8,128)}), (f32[256,768]{1,0:T(8,128)}, f32[256,256]{1,0:T(8,128)}, f32[256,1024]{1,0:T(8,128)}, ...) | async-done | bytes 3145744 | tf_op jit(solution)/shard_map/psum | solution.py:349
  351.8 2.2 broadcast_multiply_fusion.1
  354.0 1.7 broadcast_multiply_fusion.2
  356.9 1.3 copy.22
  (52 shorter events, 11.3 us)
Async XLA Ops:
  7.2 18.3 %copy-start = (f32[8,507]{1,0:T(8,128)S(1)}, f32[8,507]{1,0:T(8,128)}, u32[]{:S(2)}) copy-start(f32[8,507]{1,0:T(8,128)} %param.21) | copy-start | bytes 48676
  7.2 344.6 %all-reduce.4.cloned.1.call-start = ((), (), s32[]{:S(2)}) async-start(), calls=%async_computation | async-start | bytes 6291456 | tf_op jit(solution)/shard_map/psum | solution.py:349
  10.8 10.3 %collective-permute-start = (bf16[28,16,256]{2,1,0:T(8,128)(2,1)}, bf16[28,16,256]{2,1,0:T(8,128)(2,1)S(1)}, u32[]{:S(2)}, u32[]{:S(2)}) collective-permute-start(bf16[28,16,256]{2,1,0:T(8,128)(2,1)} %slice.76), channel_id=1, source_target_pairs={{0,15},{1,0},{2,1},{3,2},{4,3},{5,4},{6,5},{7,6},{8,7},{9,8},{10,9... | collective-permute-start | bytes 688136 | tf_op jit(solution)/shard_map/ppermute | solution.py:322
  15.0 9.4 %collective-permute-start.2 = (bf16[28,16,256]{2,1,0:T(8,128)(2,1)S(1)}, bf16[28,16,256]{2,1,0:T(8,128)(2,1)S(1)}, u32[]{:S(2)}, u32[]{:S(2)}) collective-permute-start(bf16[28,16,256]{2,1,0:T(8,128)(2,1)S(1)} %slice.79), channel_id=1, source_target_pairs={{0,15},{1,0},{2,1},{3,2},{4,3},{5,4},{6,5},{7,6},{8,7},{9,8},{10,9... | collective-permute-start | bytes 688136 | tf_op jit(solution)/shard_map/ppermute | solution.py:322
  20.9 4.6 %copy-start.7 = (s32[4096]{0:T(1024)S(1)}, s32[4096]{0:T(1024)}, u32[]{:S(2)}) copy-start(s32[4096]{0:T(1024)} %constant.4.clone) | copy-start | bytes 49156
  21.1 8.7 %copy-start.6 = (f32[768]{0:T(1024)S(1)}, f32[768]{0:T(1024)}, u32[]{:S(2)}) copy-start(f32[768]{0:T(1024)} %param.17) | copy-start | bytes 9220
  21.1 10.2 %collective-permute-start.1 = (bf16[3,128,256]{2,1,0:T(8,128)(2,1)S(1)}, bf16[3,128,256]{2,1,0:T(8,128)(2,1)S(1)}, u32[]{:S(2)}, u32[]{:S(2)}) collective-permute-start(bf16[3,128,256]{2,1,0:T(8,128)(2,1)S(1)} %slice.78), channel_id=1, source_target_pairs={{0,112},{16,0},{32,16},{48,32},{64,48},{80,64},{96,80},{112,96},{1... | collective-permute-start | bytes 589832 | tf_op jit(solution)/shard_map/ppermute | solution.py:322
  24.5 8.4 %collective-permute-start.3 = (bf16[3,128,256]{2,1,0:T(8,128)(2,1)S(1)}, bf16[3,128,256]{2,1,0:T(8,128)(2,1)S(1)}, u32[]{:S(2)}, u32[]{:S(2)}) collective-permute-start(bf16[3,128,256]{2,1,0:T(8,128)(2,1)S(1)} %slice.81), channel_id=1, source_target_pairs={{0,112},{16,0},{32,16},{48,32},{64,48},{80,64},{96,80},{112,96},{1... | collective-permute-start | bytes 589832 | tf_op jit(solution)/shard_map/ppermute | solution.py:322
  119.0 3.3 copy-start.1
  122.3 1.0 copy-start.4
  123.2 2.9 copy-start.5
  195.5 7.9 %collective-permute-start.6 = (bf16[3,128,256]{2,1,0:T(8,128)(2,1)}, bf16[3,128,256]{2,1,0:T(8,128)(2,1)}, u32[]{:S(2)}, u32[]{:S(2)}) collective-permute-start(bf16[3,128,256]{2,1,0:T(8,128)(2,1)} %slice.68), channel_id=1, source_target_pairs={{0,16},{16,32},{32,48},{48,64},{64,80},{80,96},{96,112},{112,0},{1... | collective-permute-start | bytes 589832 | tf_op jit(solution)/shard_map/ppermute | solution.py:322
  195.6 12.0 %collective-permute-start.4 = (bf16[3,128,256]{2,1,0:T(8,128)(2,1)}, bf16[3,128,256]{2,1,0:T(8,128)(2,1)S(1)}, u32[]{:S(2)}, u32[]{:S(2)}) collective-permute-start(bf16[3,128,256]{2,1,0:T(8,128)(2,1)} %slice.63), channel_id=1, source_target_pairs={{0,16},{16,32},{32,48},{48,64},{64,80},{80,96},{96,112},{112,0},{1... | collective-permute-start | bytes 589832 | tf_op jit(solution)/shard_map/ppermute | solution.py:322
  204.2 5.7 %collective-permute-start.7 = (bf16[28,16,256]{2,1,0:T(8,128)(2,1)S(1)}, bf16[28,16,256]{2,1,0:T(8,128)(2,1)S(1)}, u32[]{:S(2)}, u32[]{:S(2)}) collective-permute-start(bf16[28,16,256]{2,1,0:T(8,128)(2,1)S(1)} %pad_maximum_fusion.2), channel_id=1, source_target_pairs={{0,1},{1,2},{2,3},{3,4},{4,5},{5,6},{6,7},{7,8},{8,9},{9,10},{10,1... | collective-permute-start | bytes 688136 | tf_op jit(solution)/shard_map/ppermute | solution.py:322
  208.3 8.5 %collective-permute-start.5 = (bf16[28,16,256]{2,1,0:T(8,128)(2,1)}, bf16[28,16,256]{2,1,0:T(8,128)(2,1)}, u32[]{:S(2)}, u32[]{:S(2)}) collective-permute-start(bf16[28,16,256]{2,1,0:T(8,128)(2,1)} %pad_maximum_fusion.3), channel_id=1, source_target_pairs={{0,1},{1,2},{2,3},{3,4},{4,5},{5,6},{6,7},{7,8},{8,9},{9,10},{10,1... | collective-permute-start | bytes 688136 | tf_op jit(solution)/shard_map/ppermute | solution.py:322
  351.8 3.9 %copy-start.2 = (f32[256,1024]{1,0:T(8,128)S(1)}, f32[256,1024]{1,0:T(8,128)}, u32[]{:S(2)}) copy-start(f32[256,1024]{1,0:T(8,128)} %get-tuple-element.40) | copy-start | bytes 3145732
  351.8 3.9 %copy-start.3 = (f32[256,1024]{1,0:T(8,128)S(1)}, f32[256,1024]{1,0:T(8,128)}, u32[]{:S(2)}) copy-start(f32[256,1024]{1,0:T(8,128)} %get-tuple-element.41) | copy-start | bytes 3145732
Sparse Core Ops, SparseCore 0:
  197.3 154.4 all-reduce.3

commit v2 on v1

--- a/solution.py
+++ b/solution.py
@@ -116,7 +116,187 @@
     return jnp.concatenate(parts, 0).T[:WROWS]
 
 
-def compute(refs, s, chunk_windows=4):
+EARLY, LATE = (0, 2304), (2304, 3200)
+W_IN, W_OUT, W_PROJ, W_QKV, STRIP = slice(0, 1024), slice(1024, 2048), slice(2048, 2304), slice(2304, 3072), slice(3072, 3200)
+COLS = 3200
+MESH = pl.DeviceIdType.MESH
+
+
+def send(src, dst, sems, index, device):
+    return pltpu.make_async_remote_copy(
+        src_ref=src, dst_ref=dst, send_sem=sems[0].at[index], recv_sem=sems[1].at[index],
+        device_id=device, device_id_type=MESH,
+    )
+
+
+def greet(s):
+    barrier = pltpu.get_barrier_semaphore()
+    peers = [((s.lat + d) % 8, s.lon) for d in range(1, 8)] + [(s.lat, (s.lon + d) % 16) for d in range(1, 16)]
+    peers += [((s.lat + d) % 8, (s.lon + d) % 16) for d in (1, -1)]
+    for peer in peers:
+        pl.semaphore_signal(barrier, inc=1, device_id=peer, device_id_type=MESH)
+    pl.semaphore_wait(barrier, len(peers))
+
+
+def halo_in(s):
+    west, north = (s.lon + 15) % 16, (s.lat + 7) % 8
+    far, near = [], []
+    for n, (src, dst) in enumerate(((s.x_in, s.x), (s.g_in, s.g))):
+        near.append(pltpu.make_async_copy(src, dst.at[0:28, 0:112], s.near_sem.at[n]))
+        far.append(send(src.at[:, 0:16], dst.at[0:28, 112:128], s.halo, 3 * n, (s.lat, west)))
+        far.append(send(src.at[0:SHIFT], dst.at[28:31, 0:112], s.halo, 3 * n + 1, (north, s.lon)))
+        far.append(send(src.at[0:SHIFT, 0:16], dst.at[28:31, 112:128], s.halo, 3 * n + 2, (north, west)))
+    for copy in near:
+        copy.start()
+    greet(s)
+    for copy in far:
+        copy.start()
+    for copy in near + far:
+        copy.wait()
+
+
+def halo_out_copies(s, n):
+    east, south = (s.lon + 1) % 16, (s.lat + 1) % 8
+    return [
+        send(s.side.at[n, SHIFT:28], s.land_side.at[n, SHIFT:28], s.halo, 6 + 3 * n, (s.lat, east)),
+        send(s.foot.at[n, :, 0:112], s.land_foot.at[n], s.halo, 7 + 3 * n, (south, s.lon)),
+        send(s.foot.at[n, :, 112:128], s.land_side.at[n, 0:SHIFT], s.halo, 8 + 3 * n, (south, east)),
+    ]
+
+
+def scatter(s, src, dst, n):
+    def grid_row(r):
+        wr, a = r // WIN, r % WIN
+        y = jnp.concatenate(
+            [src[pl.ds(pl.multiple_of((wr * 8 + c) * WROWS + a * SLAB, SLAB), SLAB), :] for c in range(8)], 0
+        )
+        return dot(s.pm[...], y, TN).astype(BF)
+
+    for r in range(25, 28):
+        s.foot[n, r - 25] = grid_row(r)
+
+    def row(r, _):
+        y = grid_row(r)
+        dst[r + SHIFT] = y[:112]
+        s.side[n, r + SHIFT] = y[112:]
+        return 0
+    lax.fori_loop(0, 25, row, 0, unroll=5)
+    for copy in halo_out_copies(s, n):
+        copy.start()
+
+
+def halo_out_done(s, dst, n):
+    for copy in halo_out_copies(s, n):
+        copy.wait()
+    dst[0:SHIFT] = s.land_foot[n]
+    dst[:, 0:16] = dst[:, 0:16] + s.land_side[n]
+
+
+class Exchange:
+    def __init__(self, s, cols, number, small=False):
+        self.s, self.cols, self.sems, self.small = s, slice(*cols), s.sums[number], small
+        self.core, self.chip = s.lon % 2, s.lon // 2
+        self.half = pl.ds(pl.multiple_of(self.core * 128, 128), 128)
+        self.other = pl.ds(pl.multiple_of((1 - self.core) * 128, 128), 128)
+        self.share = pl.ds(pl.multiple_of(self.core * 128 + self.chip * 16, 16), 16)
+        self.twin = (s.lat, s.lon + 1 - 2 * self.core)
+
+    def core_copies(self):
+        s = self.s
+        out = [send(s.sent.at[self.other, self.cols], s.land_core.at[:, self.cols], self.sems, 0, self.twin)]
+        if self.small:
+            out.append(send(s.small, s.small_core, self.sems, 24, self.twin))
+        return out
+
+    def lon_copies(self):
+        s, out = self.s, []
+        for d in range(1, 8):
+            peer = (self.chip + d) % 8
+            to = (s.lat, peer * 2 + self.core)
+            rows = pl.ds(pl.multiple_of(peer * 16, 16), 16)
+            out.append(send(s.part.at[rows, self.cols], s.land_lon.at[self.chip, :, self.cols], self.sems, d, to))
+            if self.small:
+                out.append(send(s.small_lon.at[self.chip], s.small_lon.at[self.chip], self.sems, 24 + d, to))
+        return out
+
+    def lat_copies(self):
+        s, out = self.s, []
+        for d in range(1, 8):
+            to = ((s.lat + d) % 8, s.lon)
+            mine = s.land_lat.at[s.lat, :, self.cols]
+            out.append(send(mine, mine, self.sems, 8 + d, to))
+            if self.small:
+                out.append(send(s.small_lat.at[s.lat], s.small_lat.at[s.lat], self.sems, 32 + d, to))
+        return out
+
+    def gather_copies(self):
+        s, out = self.s, []
+        for d in range(1, 8):
+            to = (s.lat, ((self.chip + d) % 8) * 2 + self.core)
+            mine = s.total.at[self.share, self.cols]
+            out.append(send(mine, mine, self.sems, 16 + d, to))
+        return out
+
+    def pair_copies(self):
+        mine = self.s.total.at[self.half, self.cols]
+        return [send(mine, mine, self.sems, 16, self.twin)]
+
+    def core_start(self):
+        s = self.s
+        s.sent[self.other, self.cols] = s.acc[self.other, self.cols].astype(BF)
+        for copy in self.core_copies():
+            copy.start()
+
+    def lon_start(self):
+        s = self.s
+        for copy in self.core_copies():
+            copy.wait()
+        both = s.acc[self.half, self.cols] + s.land_core[:, self.cols].astype(F32)
+        s.acc[self.half, self.cols] = both
+        s.part[:, self.cols] = both.astype(BF)
+        if self.small:
+            s.small_lon[self.chip] = s.small[...] + s.small_core[...]
+        for copy in self.lon_copies():
+            copy.start()
+
+    def lat_start(self):
+        s = self.s
+        for copy in self.lon_copies():
+            copy.wait()
+        total = s.acc[self.share, self.cols]
+        for d in range(1, 8):
+            total += s.land_lon[(self.chip + d) % 8, :, self.cols].astype(F32)
+        s.land_lat[s.lat, :, self.cols] = total.astype(BF)
+        if self.small:
+            s.small_lat[s.lat] = sum(s.small_lon[i] for i in range(8))
+        for copy in self.lat_copies():
+            copy.start()
+
+    def gather_start(self):
+        s = self.s
+        for copy in self.lat_copies():
+            copy.wait()
+        total = s.land_lat[0, :, self.cols].astype(F32)
+        for i in range(1, 8):
+            total += s.land_lat[i, :, self.cols].astype(F32)
+        s.total[self.share, self.cols] = total.astype(BF)
+        if self.small:
+            s.small_out[...] = sum(s.small_lat[i] for i in range(8))
+        for copy in self.gather_copies():
+            copy.start()
+
+    def pair_start(self):
+        for copy in self.gather_copies():
+            copy.wait()
+        for copy in self.pair_copies():
+            copy.start()
+
+    def pair_done(self):
+        for copy in self.pair_copies():
+            copy.wait()
+
+
+def compute(s, chunk_windows=4):
     pair, group = head_masks()
     scale = np.float32(HD ** -0.5)
     CH = chunk_windows * WROWS
@@ -124,13 +304,14 @@
 
     def gather(src, dst):
         def row(r, _):
-            y = dot(s.pm[...], src[r]).astype(BF)
+            y = dot(s.pm[...], src[r + SHIFT]).astype(BF)
             wr, a = r // WIN, r % WIN
             for c in range(8):
                 dst[pl.ds(pl.multiple_of((wr * 8 + c) * WROWS + a * SLAB, SLAB), SLAB), :] = y[c * SLAB:(c + 1) * SLAB]
             return 0
         lax.fori_loop(0, 28, row, 0, unroll=2)
 
+    halo_in(s)
     gather(s.x, s.z)
     gather(s.g, s.gz)
 
@@ -150,10 +331,7 @@
         s.bias[0, j * WROWS:(j + 1) * WROWS] = full
         s.bias[1, j * WROWS:(j + 1) * WROWS] = jnp.where(cut, NEG, full)
     s.dbias[...] = jnp.zeros_like(s.dbias)
-    s.gw_in[...] = jnp.zeros_like(s.gw_in)
-    s.gw_out[...] = jnp.zeros_like(s.gw_out)
-    s.gw_qkv[...] = jnp.zeros_like(s.gw_qkv)
-    s.gw_proj[...] = jnp.zeros_like(s.gw_proj)
+    s.acc[...] = jnp.zeros_like(s.acc)
     s.small[...] = jnp.zeros_like(s.small)
 
     def forward_window(w):
@@ -189,19 +367,20 @@
         xhat2, istd2, hidden2 = layer_norm(resid, s.gains[1:2], s.shifts[1:2])
         act, slope = gelu_both(dot(hidden2, s.w_in[...]))
         act = act.astype(BF)
-        s.out[rows, :] = (resid + dot(act, s.w_out[...])).astype(BF)
+        out = (resid + dot(act, s.w_out[...])).astype(BF)
         gr = s.gz[rows, :]
-        s.gw_out[...] += dot(gr, act, TN)
+        s.gz[rows, :] = out
+        s.acc[:, W_OUT] += dot(gr, act, TN)
         gp = (dot(gr, s.w_out[...], NT) * slope).astype(BF)
-        s.gw_in[...] += dot(hidden2, gp, TN)
+        s.acc[:, W_IN] += dot(hidden2, gp, TN)
         gh = dot(gp, s.w_in[...], NT)
-        s.small[1:2, 0:C] += jnp.sum(gh * xhat2, 0, keepdims=True)
-        s.small[3:4, 0:C] += jnp.sum(gh, 0, keepdims=True)
+        s.small[1:2] += jnp.sum(gh * xhat2, 0, keepdims=True)
+        s.small[3:4] += jnp.sum(gh, 0, keepdims=True)
         gres = gr.astype(F32) + norm_backward(gh, xhat2, istd2, s.gains[1:2])
         s.gres[rows, :] = gres
         low = gres.astype(BF)
-        s.gw_proj[...] += dot(mixed, low, TN)
-        s.gm[rows, :] = dot(low, s.w_proj[...], NT).astype(BF)
+        s.acc[:, W_PROJ] += dot(mixed, low, TN)
+        s.mixed[rows, :] = dot(low, s.w_proj[...], NT).astype(BF)
         return 0
 
     lax.fori_loop(0, nwin // chunk_windows, phase_a, 0)
@@ -210,7 +389,7 @@
         rows = pl.ds(pl.multiple_of(w * WROWS, WROWS), WROWS)
         arows = pl.multiple_of(w * (HALF * WROWS), HALF * WROWS)
         q, k, v = s.p[rows, 0:C], s.p[rows, C:2 * C], s.p[rows, 2 * C:3 * C]
-        gm2 = stack_groups(s.gm[rows, :], group)
+        gm2 = stack_groups(s.mixed[rows, :], group)
         ga = dot(stack_pairs(v, pair), gm2, NT)
         lows, dlows = [], []
         for j in range(HALF):
@@ -228,8 +407,14 @@
         s.p[rows, C:2 * C] = gk
         s.p[rows, 2 * C:3 * C] = gv
 
+    scatter(s, s.gz, s.res, 0)
+    early = Exchange(s, EARLY, 0)
+    early.core_start()
+
     def phase_b(i, _):
         rows = pl.ds(pl.multiple_of(i * CH, CH), CH)
+        for at, step in ((1, early.lon_start), (3, early.lat_start), (5, early.gather_start), (7, early.pair_start)):
+            pl.when(i == at)(step)
 
         def win(w, _):
             backward_window(i * chunk_windows + 2 * w)
@@ -238,12 +423,14 @@
         lax.fori_loop(0, chunk_windows // 2, win, 0)
         xhat, istd, hidden = layer_norm(s.z[rows, :].astype(F32), s.gains[0:1], s.shifts[0:1])
         gp = s.p[rows, :]
-        s.gw_qkv[...] += dot(hidden, gp, TN)
-        s.small[4:5, :] += jnp.sum(gp.astype(F32), 0, keepdims=True)
+        s.acc[:, W_QKV] += dot(hidden, gp, TN)
+        sums = jnp.sum(gp.astype(F32), 0, keepdims=True)
+        for part in range(3):
+            s.small[4 + part:5 + part] += sums[:, part * C:(part + 1) * C]
         gh = dot(gp, s.w_qkv[...], NT)
-        s.small[0:1, 0:C] += jnp.sum(gh * xhat, 0, keepdims=True)
-        s.small[2:3, 0:C] += jnp.sum(gh, 0, keepdims=True)
-        s.gout[rows, :] = (s.gres[rows, :] + norm_backward(gh, xhat, istd, s.gains[0:1])).astype(BF)
+        s.small[0:1] += jnp.sum(gh * xhat, 0, keepdims=True)
+        s.small[2:3] += jnp.sum(gh, 0, keepdims=True)
+        s.z[rows, :] = (s.gres[rows, :] + norm_backward(gh, xhat, istd, s.gains[0:1])).astype(BF)
         return 0
 
     lax.fori_loop(0, nwin // chunk_windows, phase_b, 0)
@@ -261,97 +448,89 @@
             parts.append(jnp.zeros((SLAB, 256 - before - WROWS), F32))
             moved = jnp.concatenate(parts, 1)
             total = moved if total is None else total + moved
-        s.dstrip[h] = total
-
-    def scatter(src, dst):
-        def row(r, _):
-            wr, a = r // WIN, r % WIN
-            y = jnp.concatenate(
-                [src[pl.ds(pl.multiple_of((wr * 8 + c) * WROWS + a * SLAB, SLAB), SLAB), :] for c in range(8)], 0
-            )
-            dst[r] = dot(s.pm[...], y, TN).astype(BF)
-            return 0
-        lax.fori_loop(0, 28, row, 0, unroll=2)
-
-    scatter(s.out, s.res)
-    scatter(s.gout, s.ing)
+        for half in range(2):
+            s.acc[half * 128 + h * SLAB:half * 128 + (h + 1) * SLAB, STRIP] = total[:, half * 128:(half + 1) * 128]
+
+    late = Exchange(s, LATE, 1, small=True)
+    late.core_start()
+    scatter(s, s.z, s.ing, 1)
+    late.lon_start()
+    early.pair_done()
+    late.lat_start()
+    halo_out_done(s, s.res, 0)
+    late.gather_start()
+    halo_out_done(s, s.ing, 1)
+    late.pair_start()
+    late.pair_done()
 
 
 class Refs:
     pass
 
 
-INS = ("x", "g", "pm", "strip", "gains", "shifts", "w_qkv", "b_qkv", "w_proj", "w_in", "w_out")
-OUTS = ("res", "ing", "gw_in", "gw_out", "gw_qkv", "gw_proj", "small", "dstrip")
-SCR = ("z", "gz", "p", "att", "mixed", "out", "gout", "gres", "gm", "bias", "dbias")
+T = 32 * WROWS
+INS = ("x_in", "g_in", "pm", "strip", "gains", "shifts", "w_qkv", "b_qkv", "w_proj", "w_in", "w_out")
+OUTS = {
+    "res": ((28, 112, C), BF), "ing": ((28, 112, C), BF), "total": ((256, COLS), BF), "small_out": ((8, C), F32),
+}
+SCRATCH = {
+    "x": ((31, 128, C), BF), "g": ((31, 128, C), BF),
+    "z": ((T, C), BF), "gz": ((T, C), BF), "p": ((T, 3 * C), BF), "att": ((T * HALF, 256), F32), "mixed": ((T, C), BF),
+    "gres": ((T, C), F32), "bias": ((2, HALF * WROWS, 256), F32), "dbias": ((HALF * WROWS, 256), F32),
+    "acc": ((256, COLS), F32), "small": ((8, C), F32), "small_core": ((8, C), F32), "small_lon": ((8, 8, C), F32),
+    "small_lat": ((8, 8, C), F32), "sent": ((256, COLS), BF), "land_core": ((128, COLS), BF), "part": ((128, COLS), BF),
+    "land_lon": ((8, 16, COLS), BF), "land_lat": ((8, 16, COLS), BF),
+    "side": ((2, 28, 16, C), BF), "foot": ((2, 3, 128, C), BF), "land_side": ((2, 28, 16, C), BF),
+    "land_foot": ((2, 3, 112, C), BF),
+}
+SEMS = (2, 12, 12, 24, 24, 40, 40)
 
 
 def kernel(*refs):
     s = Refs()
-    for name, ref in zip(INS + OUTS + SCR, refs):
+    names = INS + tuple(OUTS) + tuple(SCRATCH)
+    for name, ref in zip(names, refs):
         setattr(s, name, ref)
-    s.last = lax.axis_index("lat") == lax.axis_size("lat") - 1
-    compute(refs, s)
-
-
-def fused(x, g, pm, strip, gains, shifts, w_qkv, b_qkv, w_proj, w_in, w_out):
-    T = 32 * WROWS
-    sds = jax.ShapeDtypeStruct
+    s.near_sem, h0, h1, a0, a1, b0, b1 = refs[len(names):]
+    s.halo, s.sums = (h0, h1), ((a0, a1), (b0, b1))
+    s.lat, s.lon = lax.axis_index("lat"), lax.axis_index("lon")
+    s.last = s.lat == 7
+    compute(s)
+
+
+def fused(*args):
     vm = pl.BlockSpec(memory_space=pltpu.VMEM)
     return pl.pallas_call(
         kernel,
-        out_shape=(
-            sds((28, 128, C), BF), sds((28, 128, C), BF), sds((C, FF), F32), sds((C, FF), F32),
-            sds((C, 3 * C), F32), sds((C, C), F32), sds((8, 3 * C), F32), sds((HEADS, SLAB, 256), F32),
+        out_shape=tuple(jax.ShapeDtypeStruct(*v) for v in OUTS.values()),
+        in_specs=[pl.BlockSpec(memory_space=pl.ANY)] * 2 + [vm] * (len(INS) - 2),
+        out_specs=[vm] * len(OUTS),
+        scratch_shapes=[pltpu.VMEM(*v) for v in SCRATCH.values()] + [pltpu.SemaphoreType.DMA((n,)) for n in SEMS],
+        compiler_params=pltpu.CompilerParams(
+            vmem_limit_bytes=63 * 1024 * 1024, collective_id=0, has_side_effects=True
         ),
-        in_specs=[vm] * len(INS),
-        out_specs=[vm] * len(OUTS),
-        scratch_shapes=[
-            pltpu.VMEM((T, C), BF), pltpu.VMEM((T, C), BF), pltpu.VMEM((T, 3 * C), BF),
-            pltpu.VMEM((T * HALF, 256), F32), pltpu.VMEM((T, C), BF), pltpu.VMEM((T, C), BF),
-            pltpu.VMEM((T, C), BF), pltpu.VMEM((T, C), F32), pltpu.VMEM((T, C), BF),
-            pltpu.VMEM((2, HALF * WROWS, 256), F32), pltpu.VMEM((HALF * WROWS, 256), F32),
-        ],
-        compiler_params=pltpu.CompilerParams(vmem_limit_bytes=60 * 1024 * 1024),
         name="windows",
-    )(x, g, pm, strip, gains, shifts, w_qkv, b_qkv, w_proj, w_in, w_out)
-
-
-def shifted(value, axis, steps):
-    count = lax.axis_size(axis)
-    return lax.ppermute(value, axis, [(i, (i + steps) % count) for i in range(count)])
-
-
-def roll_in(block):
-    wide = jnp.concatenate([block, shifted(block[:, :16], "lon", -1)], 1)
-    return jnp.concatenate([wide[SHIFT:], shifted(wide[:SHIFT], "lat", -1)], 0)
-
-
-def roll_out(block):
-    tall = jnp.concatenate([shifted(block[-SHIFT:], "lat", 1), block[:-SHIFT]], 0)
-    got = shifted(tall[:, 112:], "lon", 1)
-    return jnp.concatenate([tall[:, :16] + got, tall[:, 16:112]], 1)
+    )(*args)
 
 
 def local(tokens, out_grad, gains, shifts, w_qkv, b_qkv, w_proj, w_in, w_out, rel_bias):
     rows_n, cols_n, levels, channels = tokens.shape
-    total = rows_n * lax.axis_size("lat") * cols_n * lax.axis_size("lon") * levels
-    x = roll_in(tokens.reshape(rows_n, cols_n * levels, channels))
-    g = roll_in(out_grad.reshape(rows_n, cols_n * levels, channels))
+    scale = float(rows_n * lax.axis_size("lat") * cols_n * lax.axis_size("lon") * levels) ** -0.5
     index = jnp.asarray(strip_map().reshape(-1))
     onehot = (index[:, None] == jnp.arange(NREL, dtype=jnp.int32)[None, :]).astype(F32)
     strip = lax.dot_general(rel_bias, onehot, NT, precision=lax.Precision.HIGHEST).reshape(HEADS, SLAB, 256)
     pm = jnp.asarray(placement(), BF)
-    res, ing, gw_in, gw_out, gw_qkv, gw_proj, small, dstrip = fused(
-        x, g, pm, strip, gains, shifts, w_qkv, b_qkv[None], w_proj, w_in, w_out
+    flat = (rows_n, cols_n * levels, channels)
+    res, ing, total, small = fused(
+        tokens.reshape(flat), out_grad.reshape(flat), pm, strip, gains, shifts, w_qkv, b_qkv[None], w_proj, w_in, w_out
     )
-    table = lax.dot_general(dstrip.reshape(HEADS, -1), onehot, NN, precision=lax.Precision.HIGHEST)
-    sums = lax.psum((gw_in, gw_out, gw_qkv, gw_proj, small, table), ("lat", "lon"))
-    gw_in, gw_out, gw_qkv, gw_proj, small, table = [v * float(total) ** -0.5 for v in sums]
-    shape = tokens.shape
+    total = total.astype(F32) * scale
+    small = small * scale
+    dstrip = total[:, STRIP].reshape(2, HEADS, SLAB, 128).transpose(1, 2, 0, 3).reshape(HEADS, -1)
+    table = lax.dot_general(dstrip, onehot, NN, precision=lax.Precision.HIGHEST)
     return (
-        roll_out(res).reshape(shape), roll_out(ing).reshape(shape),
-        small[0:2, :C], small[2:4, :C], gw_qkv, small[4], gw_proj, gw_in, gw_out.T, table,
+        res.reshape(tokens.shape), ing.reshape(tokens.shape), small[0:2], small[2:4], total[:, W_QKV],
+        small[4:7].reshape(3 * C), total[:, W_PROJ], total[:, W_IN], total[:, W_OUT].T, table,
     )
 
 

time: 366 us -> 167 us (0.46)
  waiting for transfers between devices: 138 us -> 0 us
  blocking collectives: 69.5 us -> 0 us
  Pallas kernels: 84.8 us -> 137 us
  starting transfers between devices: 17.2 us -> 0 us
  between operations: 14.3 us -> 0.72 us
  other arithmetic: 14.1 us -> 1.68 us
    psum x1 -> x0, waiting for transfers between devices: 132 us -> none  [local(): lax.psum((gw_in, gw_out, gw_qkv, gw_proj, small, table), ('lat', 'lon'))]
    psum x1 -> x0, blocking collectives: 69.5 us -> none  [local(): lax.psum((gw_in, gw_out, gw_qkv, gw_proj, small, table), ('lat', 'lon'))]
    pallas_call x1, Pallas kernels: 84.8 us -> 137 us  [fused(): pl.pallas_call(kernel, out_shape=tuple((jax.ShapeDtypeStruct(*v) for v in...]
    ppermute x8 -> x0, starting transfers between devices: 17.2 us -> none  [shifted(): lax.ppermute(value, axis, [(i, (i + steps) % count) for i in range(count)])]
    ppermute x8 -> x0, waiting for transfers between devices: 5.2 us -> none  [shifted(): lax.ppermute(value, axis, [(i, (i + steps) % count) for i in range(count)])]
    concatenate x4 -> x0, other arithmetic: 5.13 us -> none  [the longest x2 2.82 us: roll_in(): return jnp.concatenate([wide[SHIFT:], shifted(wide[:SHIFT], 'lat', -1)], 0)]
    slice x12 -> x5, local copies, waits for them, and re-layouts: 6.28 us -> 2.25 us  [the longest x1 0.93 us: local(): total[:, W_QKV]]
    reshape x4 -> x7, local copies, waits for them, and re-layouts: 10.8 us -> 8.82 us  [the longest x1 4 us: local(): res.reshape(tokens.shape)]
  transfers between devices with their start and end apart: 9 -> 0, of which waited for: 2 -> 0; matrix products, arithmetic and copies ran while one was open for 6% -> 0% of each run, Pallas kernels for 0% -> 0%
where the time goes in v2:
time: 167 us; the launch traced here: 166 us
  Pallas kernels  137 us (82%)
  local copies, waits for them, and re-layouts  17.3 us (10%)
  matrix products  9.13 us (5%)
  other arithmetic  1.68 us (1%)
    pallas_call x1, Pallas kernels, fused(): pl.pallas_call(kernel, out_shape=tuple((jax.ShapeDtypeStruct(*v) for v in...  137 us
    dot_general x1, matrix products, local(): lax.dot_general(rel_bias, onehot, NT, precision=lax.Precision.HIGHEST)  5.1 us
    dot_general x1, matrix products, local(): table = lax.dot_general(dstrip, onehot, NN, precision=lax.Precision.HIGHEST)  4.03 us
    reshape x1, local copies, waits for them, and re-layouts, local(): res.reshape(tokens.shape)  4 us

profile of v2, /device:TPU:1, one launch (start us, length us, event | category | flops | bytes accessed | tf_op | source)
XLA Modules:
  0.0 166.2 jit_solution(11942531095632532385)
XLA Ops:
  0.6 0.0 copy-start
  0.7 0.0 copy-start.1
  0.7 1.4 broadcast_in_dim.2.refs_7_
  2.1 0.0 copy-done
  2.1 5.1 %fusion.1 = f32[4096,8]{0,1:T(8,128)S(1)} fusion(f32[8,507]{1,0:T(8,128)S(1)} %copy-done, s32[4096]{0:T(1024)} %constant.2.clone), kind=kOutput, calls=%fused_computation.2 | convolution fusion | flops 201437184 | bytes 163680 | tf_op jit(solution)/shard_map/dot_general | solution.py:521
  7.2 0.7 copy.28
  7.9 0.0 copy-done.1
  7.9 1.3 reshape.45.refs_0_
  9.2 0.0 copy-done.2
  9.2 1.3 reshape.46.refs_1_
  10.6 137.4 %windows.1 = (bf16[28,112,256]{2,1,0:T(8,128)(2,1)}, bf16[28,112,256]{2,1,0:T(8,128)(2,1)}, bf16[256,3200]{1,0:T(8,128)(2,1)}, f32[8,256]{1,0:T(8,128)}) custom-call(bf16[28,112,256]{2,1,0:T(8,128)(2,1)} %reshape.45.refs_0_, bf16[28,112,256]{2,1,0:T(8,128)(2,1)} %reshape.46.refs_1_, bf16[128,128]{1,0:T(8,128)(2,1)} %constant.8.clone.refs_2_, ...), custom_call_target="tpu_custom_call" | custom-call | tf_op jit(solution)/shard_map/windows/pallas_call | solution.py:503
  147.9 0.0 copy-start.4
  147.9 4.0 %reshape.48 = bf16[28,28,4,256]{3,2,1,0:T(4,128)(2,1)} reshape(bf16[28,112,256]{2,1,0:T(8,128)(2,1)} %get-tuple-element.14) | data formatting | bytes 3211264 | tf_op jit(solution)/shard_map/reshape | solution.py:532
  152.0 0.6 fusion.4
  152.5 0.6 reshape.50
  153.1 1.3 reshape.49
  154.5 1.7 %convert_multiply_fusion = f32[256,3200]{1,0:T(8,128)S(1)} fusion(bf16[256,3200]{1,0:T(8,128)(2,1)} %get-tuple-element.17), kind=kLoop, calls=%fused_computation.5 | loop fusion | flops 1638400 | bytes 4915200 | tf_op jit(solution)/shard_map/mul | solution.py:527
  156.2 0.1 copy.29
  156.3 0.1 reshape.52
  156.4 4.0 %fusion = f32[8,507]{1,0:T(8,128)} fusion(f32[8,4096]{1,0:T(8,128)S(1)} %reshape.52, s32[4096]{0:T(1024)} %constant.2.clone), kind=kOutput, calls=%fused_computation.1 | convolution fusion | flops 201437184 | bytes 163680 | tf_op jit(solution)/shard_map/dot_general | solution.py:530
  160.4 0.7 slice.36
  161.2 0.9 slice.34
  162.1 1.6 slice_bitcast_fusion
  163.7 2.5 %copy.24 = f32[1024,256]{1,0:T(8,128)} copy(f32[1024,256]{0,1:T(8,128)} %get-tuple-element.38) | data formatting | bytes 2097152
  (7 shorter events, 0.0 us)
Async XLA Ops:
  0.6 1.4 copy-start
  0.7 7.2 %copy-start.1 = (bf16[28,28,4,256]{3,2,1,0:T(4,128)(2,1)S(1)}, bf16[28,28,4,256]{3,2,1,0:T(4,128)(2,1)}, u32[]{:S(2)}) copy-start(bf16[28,28,4,256]{3,2,1,0:T(4,128)(2,1)} %param.12) | copy-start | bytes 4816900
  7.2 2.1 %copy-start.2 = (bf16[28,28,4,256]{3,2,1,0:T(4,128)(2,1)S(1)}, bf16[28,28,4,256]{3,2,1,0:T(4,128)(2,1)}, u32[]{:S(2)}) copy-start(bf16[28,28,4,256]{3,2,1,0:T(4,128)(2,1)} %param.13) | copy-start | bytes 4816900
  147.9 4.0 %copy-start.4 = (f32[8,256]{1,0:T(8,128)S(1)}, f32[8,256]{1,0:T(8,128)}, u32[]{:S(2)}) copy-start(f32[8,256]{1,0:T(8,128)} %get-tuple-element.16) | copy-start | bytes 24580
  147.9 5.2 %copy-start.3 = (bf16[28,112,256]{2,1,0:T(8,128)(2,1)S(1)}, bf16[28,112,256]{2,1,0:T(8,128)(2,1)}, u32[]{:S(2)}) copy-start(bf16[28,112,256]{2,1,0:T(8,128)(2,1)} %get-tuple-element.15) | copy-start | bytes 4816900

commit v3 on v2

--- a/solution.py
+++ b/solution.py
@@ -116,9 +116,10 @@
     return jnp.concatenate(parts, 0).T[:WROWS]
 
 
-EARLY, LATE = (0, 2304), (2304, 3200)
-W_IN, W_OUT, W_PROJ, W_QKV, STRIP = slice(0, 1024), slice(1024, 2048), slice(2048, 2304), slice(2304, 3072), slice(3072, 3200)
-COLS = 3200
+FIRST, SECOND, LATE = (0, 1024), (1024, 2304), (2304, 3072)
+W_IN, W_PROJ, W_QKV = slice(0, 1024), slice(2048, 2304), slice(2304, 3072)
+COLS = 3072
+LOG2E = np.float32(1.4426950408889634)
 MESH = pl.DeviceIdType.MESH
 
 
@@ -138,58 +139,208 @@
     pl.semaphore_wait(barrier, len(peers))
 
 
-def halo_in(s):
+def near_copies(s):
+    return [
+        pltpu.make_async_copy(src, dst.at[0:28, 0:28], s.near_sem.at[n])
+        for n, (src, dst) in enumerate(((s.x_in, s.x), (s.g_in, s.g)))
+    ]
+
+
+def halo_in_copies(s):
     west, north = (s.lon + 15) % 16, (s.lat + 7) % 8
-    far, near = [], []
+    far = []
     for n, (src, dst) in enumerate(((s.x_in, s.x), (s.g_in, s.g))):
-        near.append(pltpu.make_async_copy(src, dst.at[0:28, 0:112], s.near_sem.at[n]))
-        far.append(send(src.at[:, 0:16], dst.at[0:28, 112:128], s.halo, 3 * n, (s.lat, west)))
-        far.append(send(src.at[0:SHIFT], dst.at[28:31, 0:112], s.halo, 3 * n + 1, (north, s.lon)))
-        far.append(send(src.at[0:SHIFT, 0:16], dst.at[28:31, 112:128], s.halo, 3 * n + 2, (north, west)))
-    for copy in near:
+        far.append(send(src.at[:, 0:4], dst.at[0:28, 28:32], s.halo, 3 * n, (s.lat, west)))
+        far.append(send(src.at[0:SHIFT], dst.at[28:31, 0:28], s.halo, 3 * n + 1, (north, s.lon)))
+        far.append(send(src.at[0:SHIFT, 0:4], dst.at[28:31, 28:32], s.halo, 3 * n + 2, (north, west)))
+    return far
+
+
+def halo_start(s):
+    for copy in near_copies(s):
         copy.start()
     greet(s)
-    for copy in far:
+    for copy in halo_in_copies(s):
         copy.start()
-    for copy in near + far:
+
+
+def near_done(s):
+    for copy in near_copies(s):
         copy.wait()
+
+
+def halo_in_done(s):
+    for copy in halo_in_copies(s):
+        copy.wait()
+
+
+def slab(wr, c, a):
+    return pl.ds(pl.multiple_of((wr * 8 + c) * WROWS + a * SLAB, SLAB), SLAB)
+
+
+def gather_own(s, src, dst):
+    def row(r, _):
+        y = dot(s.pm[0:96, 0:112], src[r + SHIFT, 0:28].reshape(112, C)).astype(BF)
+        for c in range(6):
+            dst[slab(r // WIN, c, r % WIN), :] = y[c * SLAB:(c + 1) * SLAB]
+        return 0
+    lax.fori_loop(0, 25, row, 0, unroll=5)
+
+
+def gather_rest(s, src, dst):
+    def row(r, _):
+        y = dot(s.pm[96:128], src[r + SHIFT].reshape(128, C)).astype(BF)
+        for c in range(2):
+            dst[slab(r // WIN, 6 + c, r % WIN), :] = y[c * SLAB:(c + 1) * SLAB]
+        return 0
+    lax.fori_loop(0, 25, row, 0, unroll=5)
+    for r in range(25, 28):
+        y = dot(s.pm[...], src[r + SHIFT].reshape(128, C)).astype(BF)
+        for c in range(8):
+            dst[slab(r // WIN, c, r % WIN), :] = y[c * SLAB:(c + 1) * SLAB]
 
 
 def halo_out_copies(s, n):
     east, south = (s.lon + 1) % 16, (s.lat + 1) % 8
     return [
         send(s.side.at[n, SHIFT:28], s.land_side.at[n, SHIFT:28], s.halo, 6 + 3 * n, (s.lat, east)),
-        send(s.foot.at[n, :, 0:112], s.land_foot.at[n], s.halo, 7 + 3 * n, (south, s.lon)),
-        send(s.foot.at[n, :, 112:128], s.land_side.at[n, 0:SHIFT], s.halo, 8 + 3 * n, (south, east)),
+        send(s.foot.at[n, :, 0:28], s.land_foot.at[n], s.halo, 7 + 3 * n, (south, s.lon)),
+        send(s.foot.at[n, :, 28:32], s.land_side.at[n, 0:SHIFT], s.halo, 8 + 3 * n, (south, east)),
     ]
 
 
-def scatter(s, src, dst, n):
-    def grid_row(r):
-        wr, a = r // WIN, r % WIN
-        y = jnp.concatenate(
-            [src[pl.ds(pl.multiple_of((wr * 8 + c) * WROWS + a * SLAB, SLAB), SLAB), :] for c in range(8)], 0
-        )
-        return dot(s.pm[...], y, TN).astype(BF)
-
+def grid_row(s, src, r, low, high):
+    y = jnp.concatenate([src[slab(r // WIN, c, r % WIN), :] for c in range(low, high)], 0)
+    return dot(s.pm[low * SLAB:high * SLAB], y, TN).astype(BF).reshape(32, LEV, C)
+
+
+def scatter_foot(s, src, n):
     for r in range(25, 28):
-        s.foot[n, r - 25] = grid_row(r)
+        s.foot[n, r - 25] = grid_row(s, src, r, 0, 8)
+
+
+def scatter_all(s, src, dst, n):
+    scatter_foot(s, src, n)
 
     def row(r, _):
-        y = grid_row(r)
-        dst[r + SHIFT] = y[:112]
-        s.side[n, r + SHIFT] = y[112:]
+        y = grid_row(s, src, r, 0, 8)
+        dst[r + SHIFT] = y[:28]
+        s.side[n, r + SHIFT] = y[28:]
         return 0
     lax.fori_loop(0, 25, row, 0, unroll=5)
     for copy in halo_out_copies(s, n):
         copy.start()
+
+
+def scatter_sent(s, src, dst, n):
+    scatter_foot(s, src, n)
+
+    def row(r, _):
+        y = grid_row(s, src, r, 4, 8)
+        dst[r + SHIFT] = y[:28]
+        s.side[n, r + SHIFT] = y[28:]
+        return 0
+    lax.fori_loop(0, 25, row, 0, unroll=5)
+    for copy in halo_out_copies(s, n):
+        copy.start()
+
+
+def scatter_own(s, src, dst):
+    def row(r, _):
+        y = grid_row(s, src, r, 0, 4)
+        dst[r + SHIFT, 0:16] = y[:16]
+        seam = dst[r + SHIFT, 16:20].reshape(16, C) + y[16:20].reshape(16, C)
+        dst[r + SHIFT, 16:20] = seam.reshape(4, LEV, C)
+        return 0
+    lax.fori_loop(0, 25, row, 0, unroll=5)
 
 
 def halo_out_done(s, dst, n):
     for copy in halo_out_copies(s, n):
         copy.wait()
     dst[0:SHIFT] = s.land_foot[n]
-    dst[:, 0:16] = dst[:, 0:16] + s.land_side[n]
+
+    def row(r, _):
+        both = dst[r, 0:4].reshape(16, C) + s.land_side[n, r].reshape(16, C)
+        dst[r, 0:4] = both.reshape(4, LEV, C)
+        return 0
+    lax.fori_loop(0, 28, row, 0, unroll=7)
+
+
+def thirds(value):
+    high = value.astype(BF)
+    rest = value - high.astype(F32)
+    mid = rest.astype(BF)
+    return jnp.concatenate([v.astype(F32) for v in (high, mid, (rest - mid.astype(F32)))], 0).astype(BF)
+
+
+def chosen(s, i):
+    slots = lax.broadcasted_iota(jnp.int32, (512, 256), 0)
+    return jnp.where(slots == s.index[i:i + 1, :], 1.0, 0.0).astype(BF)
+
+
+def expand_table(s):
+    s.rel[...] = jnp.zeros_like(s.rel)
+    s.rel[:, 0:NREL] = s.rel_bias[...]
+    table = thirds(s.rel[...])
+    s.strip[...] = jnp.zeros_like(s.strip)
+    for i in range(WIN * WLEV):
+        out = dot(table, chosen(s, i))
+        s.strip[i] = out[0:8] + out[8:16] + out[16:24]
+
+
+def collect_table(s):
+    for h in range(HEADS):
+        j, g = h % HALF, h // HALF
+        total = None
+        for ak in range(WIN):
+            piece = s.dbias[j * WROWS + ak * SLAB:j * WROWS + (ak + 1) * SLAB, g * 128:g * 128 + WROWS]
+            before = (6 - ak) * SLAB
+            parts = [jnp.zeros((SLAB, before), F32)] if before else []
+            moved = jnp.concatenate(parts + [piece, jnp.zeros((SLAB, 256 - before - WROWS), F32)], 1)
+            total = moved if total is None else total + moved
+        s.dstrip[h] = total
+    table = None
+    for i in range(WIN * WLEV):
+        part = dot(thirds(s.dstrip[:, i, :]), chosen(s, i), NT)
+        table = part if table is None else table + part
+    table = table[0:8] + table[8:16] + table[16:24]
+    s.small[0:8] = table[:, 0:256]
+    s.small[8:16] = table[:, 256:512]
+
+
+def tail_lon_copies(s):
+    mine, out = s.tail_lon.at[s.lon], []
+    for d in range(1, 16):
+        out.append(send(mine, mine, s.tails, d, (s.lat, (s.lon + d) % 16)))
+    return out
+
+
+def tail_lat_copies(s):
+    mine, out = s.tail_lat.at[s.lat], []
+    for d in range(1, 8):
+        out.append(send(mine, mine, s.tails, 15 + d, ((s.lat + d) % 8, s.lon)))
+    return out
+
+
+def tail_lon_start(s):
+    s.tail_lon[s.lon] = s.tail[...]
+    for copy in tail_lon_copies(s):
+        copy.start()
+
+
+def tail_lat_start(s):
+    for copy in tail_lon_copies(s):
+        copy.wait()
+    s.tail_lat[s.lat] = sum(s.tail_lon[i] for i in range(16))
+    for copy in tail_lat_copies(s):
+        copy.start()
+
+
+def tail_done(s):
+    for copy in tail_lat_copies(s):
+        copy.wait()
+    s.tail_out[...] = sum(s.tail_lat[i] for i in range(8))
 
 
 class Exchange:
@@ -302,19 +453,9 @@
     CH = chunk_windows * WROWS
     nwin = 32
 
-    def gather(src, dst):
-        def row(r, _):
-            y = dot(s.pm[...], src[r + SHIFT]).astype(BF)
-            wr, a = r // WIN, r % WIN
-            for c in range(8):
-                dst[pl.ds(pl.multiple_of((wr * 8 + c) * WROWS + a * SLAB, SLAB), SLAB), :] = y[c * SLAB:(c + 1) * SLAB]
-            return 0
-        lax.fori_loop(0, 28, row, 0, unroll=2)
-
-    halo_in(s)
-    gather(s.x, s.z)
-    gather(s.g, s.gz)
-
+    halo_start(s)
+
+    expand_table(s)
     key_row = lax.broadcasted_iota(jnp.int32, (WROWS, 256), 0)
     lane = lax.broadcasted_iota(jnp.int32, (WROWS, 256), 1)
     qa, ka = (lane % 128) // SLAB, key_row // SLAB
@@ -323,7 +464,7 @@
     for j in range(HALF):
         tiles = []
         for g in range(2):
-            strip = s.strip[j + HALF * g]
+            strip = s.strip[:, j + HALF * g, :] * LOG2E
             rows = [strip[:, (6 - ak) * SLAB:(6 - ak) * SLAB + WROWS] for ak in range(WIN)]
             tile = jnp.concatenate(rows, 0)
             tiles.append(jnp.concatenate([tile, jnp.zeros((WROWS, 128 - WROWS), F32)], 1))
@@ -331,8 +472,17 @@
         s.bias[0, j * WROWS:(j + 1) * WROWS] = full
         s.bias[1, j * WROWS:(j + 1) * WROWS] = jnp.where(cut, NEG, full)
     s.dbias[...] = jnp.zeros_like(s.dbias)
+    s.tail[...] = jnp.zeros_like(s.tail)
     s.acc[...] = jnp.zeros_like(s.acc)
     s.small[...] = jnp.zeros_like(s.small)
+    near_done(s)
+    for src, dst in ((s.x, s.z), (s.g, s.gz)):
+        gather_own(s, src, dst)
+
+    def rest():
+        halo_in_done(s)
+        for src, dst in ((s.x, s.z), (s.g, s.gz)):
+            gather_rest(s, src, dst)
 
     def forward_window(w):
         rows = pl.ds(pl.multiple_of(w * WROWS, WROWS), WROWS)
@@ -343,39 +493,47 @@
         vt = v.T
         lows = []
         for j in range(HALF):
-            t = scores[j * WROWS:(j + 1) * WROWS] * scale + s.bias[which, j * WROWS:(j + 1) * WROWS]
-            e = jnp.exp(t - jnp.max(t, 0, keepdims=True))
+            t = scores[j * WROWS:(j + 1) * WROWS] * (scale * LOG2E) + s.bias[which, j * WROWS:(j + 1) * WROWS]
+            e = jnp.exp2(t - jnp.max(t, 0, keepdims=True))
             att = e * (1.0 / jnp.sum(e, 0, keepdims=True))
-            s.att[pl.ds(arows + j * WROWS, WROWS), :] = att
-            lows.append(att.astype(BF))
+            low = att.astype(BF)
+            s.att[pl.ds(arows + j * WROWS, WROWS), :] = low
+            lows.append(low)
         s.mixed[rows, :] = down_keys(vt, jnp.concatenate(lows, 0)).astype(BF)
 
-    def phase_a(i, _):
+    def phase_a(step, _):
+        i = jnp.where(step < 3, 2 * step, jnp.where(step < 6, 2 * step - 5, step))
+        pl.when(step == 3)(rest)
         rows = pl.ds(pl.multiple_of(i * CH, CH), CH)
         x = s.z[rows, :].astype(F32)
         _, _, hidden1 = layer_norm(x, s.gains[0:1], s.shifts[0:1])
         s.p[rows, :] = (dot(hidden1, s.w_qkv[...]) + s.b_qkv[...]).astype(BF)
 
         def win(w, _):
-            forward_window(i * chunk_windows + 2 * w)
-            forward_window(i * chunk_windows + 2 * w + 1)
+            for u in range(4):
+                forward_window(i * chunk_windows + 4 * w + u)
             return 0
-        lax.fori_loop(0, chunk_windows // 2, win, 0)
+        lax.fori_loop(0, chunk_windows // 4, win, 0)
 
         mixed = s.mixed[rows, :]
         resid = s.z[rows, :].astype(F32) + dot(mixed, s.w_proj[...])
         xhat2, istd2, hidden2 = layer_norm(resid, s.gains[1:2], s.shifts[1:2])
-        act, slope = gelu_both(dot(hidden2, s.w_in[...]))
-        act = act.astype(BF)
-        out = (resid + dot(act, s.w_out[...])).astype(BF)
         gr = s.gz[rows, :]
-        s.gz[rows, :] = out
-        s.acc[:, W_OUT] += dot(gr, act, TN)
-        gp = (dot(gr, s.w_out[...], NT) * slope).astype(BF)
-        s.acc[:, W_IN] += dot(hidden2, gp, TN)
-        gh = dot(gp, s.w_in[...], NT)
-        s.small[1:2] += jnp.sum(gh * xhat2, 0, keepdims=True)
-        s.small[3:4] += jnp.sum(gh, 0, keepdims=True)
+        gr_t, hid_t = gr.T, hidden2.T
+        out, gh = resid, None
+        for f in range(4):
+            cols = slice(f * 256, f * 256 + 256)
+            act, slope = gelu_both(dot(hidden2, s.w_in[:, cols]))
+            act = act.astype(BF)
+            out = out + dot(act, s.w_out[cols, :])
+            s.acc[:, 1024 + f * 256:1280 + f * 256] += dot(gr_t, act)
+            gp = (dot(gr, s.w_out[cols, :], NT) * slope).astype(BF)
+            s.acc[:, cols] += dot(hid_t, gp)
+            part = dot(gp, s.w_in[:, cols], NT)
+            gh = part if gh is None else gh + part
+        s.gz[rows, :] = out.astype(BF)
+        s.small[19:20] += jnp.sum(gh * xhat2, 0, keepdims=True)
+        s.small[20:21] += jnp.sum(gh, 0, keepdims=True)
         gres = gr.astype(F32) + norm_backward(gh, xhat2, istd2, s.gains[1:2])
         s.gres[rows, :] = gres
         low = gres.astype(BF)
@@ -383,7 +541,14 @@
         s.mixed[rows, :] = dot(low, s.w_proj[...], NT).astype(BF)
         return 0
 
-    lax.fori_loop(0, nwin // chunk_windows, phase_a, 0)
+    lax.fori_loop(0, 8, phase_a, 0)
+    for f in range(4):
+        cols = slice(1024 + f * 256, 1280 + f * 256)
+        s.acc[:, cols] = s.acc[:, cols].T
+    first, second, late = Exchange(s, FIRST, 0), Exchange(s, SECOND, 1), Exchange(s, LATE, 2, small=True)
+    first.core_start()
+    second.core_start()
+    scatter_all(s, s.gz, s.res, 0)
 
     def backward_window(w):
         rows = pl.ds(pl.multiple_of(w * WROWS, WROWS), WROWS)
@@ -393,11 +558,12 @@
         ga = dot(stack_pairs(v, pair), gm2, NT)
         lows, dlows = [], []
         for j in range(HALF):
-            att = s.att[pl.ds(arows + j * WROWS, WROWS), :]
+            low = s.att[pl.ds(arows + j * WROWS, WROWS), :]
+            att = low.astype(F32)
             t = att * ga[j * WROWS:(j + 1) * WROWS]
             ds = t - att * jnp.sum(t, 0, keepdims=True)
             s.dbias[j * WROWS:(j + 1) * WROWS] += ds
-            lows.append(att.astype(BF))
+            lows.append(low)
             dlows.append((ds * scale).astype(BF))
         low, dlow = jnp.concatenate(lows, 0), jnp.concatenate(dlows, 0)
         gv = pick_pairs(dot(low, gm2), pair).astype(BF)
@@ -407,61 +573,63 @@
         s.p[rows, C:2 * C] = gk
         s.p[rows, 2 * C:3 * C] = gv
 
-    scatter(s, s.gz, s.res, 0)
-    early = Exchange(s, EARLY, 0)
-    early.core_start()
-
     def phase_b(i, _):
         rows = pl.ds(pl.multiple_of(i * CH, CH), CH)
-        for at, step in ((1, early.lon_start), (3, early.lat_start), (5, early.gather_start), (7, early.pair_start)):
-            pl.when(i == at)(step)
+        steps = (
+            first.lon_start, second.lon_start, first.lat_start, second.lat_start,
+            first.gather_start, second.gather_start, first.pair_start,
+        )
+        for at, step in enumerate(steps):
+            pl.when(i == at + 1)(step)
 
         def win(w, _):
-            backward_window(i * chunk_windows + 2 * w)
-            backward_window(i * chunk_windows + 2 * w + 1)
+            for u in range(4):
+                backward_window(i * chunk_windows + 4 * w + u)
             return 0
-        lax.fori_loop(0, chunk_windows // 2, win, 0)
-        xhat, istd, hidden = layer_norm(s.z[rows, :].astype(F32), s.gains[0:1], s.shifts[0:1])
+        lax.fori_loop(0, chunk_windows // 4, win, 0)
+        _, _, hidden = layer_norm(s.z[rows, :].astype(F32), s.gains[0:1], s.shifts[0:1])
         gp = s.p[rows, :]
         s.acc[:, W_QKV] += dot(hidden, gp, TN)
         sums = jnp.sum(gp.astype(F32), 0, keepdims=True)
         for part in range(3):
-            s.small[4 + part:5 + part] += sums[:, part * C:(part + 1) * C]
-        gh = dot(gp, s.w_qkv[...], NT)
-        s.small[0:1] += jnp.sum(gh * xhat, 0, keepdims=True)
-        s.small[2:3] += jnp.sum(gh, 0, keepdims=True)
+            s.small[16 + part:17 + part] += sums[:, part * C:(part + 1) * C]
+        return 0
+
+    lax.fori_loop(0, 8, phase_b, 0)
+    collect_table(s)
+    late.core_start()
+    halo_out_done(s, s.res, 0)
+
+    def phase_c(step, _):
+        i = jnp.where(step < 2, 7 - step, jnp.where(step < 5, 9 - 2 * step, 14 - 2 * step))
+        for at, action in (
+            (2, late.lon_start), (3, second.pair_start), (5, lambda: scatter_sent(s, s.z, s.ing, 1)), (6, late.lat_start),
+        ):
+            pl.when(step == at)(action)
+        rows = pl.ds(pl.multiple_of(i * CH, CH), CH)
+        xhat, istd, _ = layer_norm(s.z[rows, :].astype(F32), s.gains[0:1], s.shifts[0:1])
+        gh = dot(s.p[rows, :], s.w_qkv[...], NT)
+        s.tail[0:1] += jnp.sum(gh * xhat, 0, keepdims=True)
+        s.tail[1:2] += jnp.sum(gh, 0, keepdims=True)
         s.z[rows, :] = (s.gres[rows, :] + norm_backward(gh, xhat, istd, s.gains[0:1])).astype(BF)
         return 0
 
-    lax.fori_loop(0, nwin // chunk_windows, phase_b, 0)
-
-    for h in range(HEADS):
-        j, g = h % HALF, h // HALF
-        total = None
-        for ak in range(WIN):
-            piece = s.dbias[j * WROWS + ak * SLAB:j * WROWS + (ak + 1) * SLAB, g * 128:g * 128 + WROWS]
-            before = (6 - ak) * SLAB
-            parts = []
-            if before:
-                parts.append(jnp.zeros((SLAB, before), F32))
-            parts.append(piece)
-            parts.append(jnp.zeros((SLAB, 256 - before - WROWS), F32))
-            moved = jnp.concatenate(parts, 1)
-            total = moved if total is None else total + moved
-        for half in range(2):
-            s.acc[half * 128 + h * SLAB:half * 128 + (h + 1) * SLAB, STRIP] = total[:, half * 128:(half + 1) * 128]
-
-    late = Exchange(s, LATE, 1, small=True)
-    late.core_start()
-    scatter(s, s.z, s.ing, 1)
-    late.lon_start()
-    early.pair_done()
-    late.lat_start()
-    halo_out_done(s, s.res, 0)
+    lax.fori_loop(0, 8, phase_c, 0)
+    tail_lon_start(s)
+    scatter_own(s, s.z, s.ing)
     late.gather_start()
+    tail_lat_start(s)
+    first.pair_done()
+    second.pair_done()
+    s.o_in[...] = s.total[:, W_IN]
+    for f in range(4):
+        s.o_out[f * 256:(f + 1) * 256] = s.total[:, 1024 + f * 256:1280 + f * 256]
+    s.o_proj[...] = s.total[:, W_PROJ]
     halo_out_done(s, s.ing, 1)
     late.pair_start()
+    tail_done(s)
     late.pair_done()
+    s.o_qkv[...] = s.total[:, W_QKV]
 
 
 class Refs:
@@ -469,21 +637,25 @@
 
 
 T = 32 * WROWS
-INS = ("x_in", "g_in", "pm", "strip", "gains", "shifts", "w_qkv", "b_qkv", "w_proj", "w_in", "w_out")
+GRID = (LEV, C)
+INS = ("x_in", "g_in", "pm", "index", "gains", "shifts", "w_qkv", "b_qkv", "w_proj", "w_in", "w_out", "rel_bias")
 OUTS = {
-    "res": ((28, 112, C), BF), "ing": ((28, 112, C), BF), "total": ((256, COLS), BF), "small_out": ((8, C), F32),
+    "res": ((28, 28) + GRID, BF), "ing": ((28, 28) + GRID, BF), "o_in": ((C, FF), BF), "o_out": ((FF, C), BF),
+    "o_qkv": ((C, 3 * C), BF), "o_proj": ((C, C), BF), "small_out": ((24, C), F32), "tail_out": ((8, C), F32),
 }
 SCRATCH = {
-    "x": ((31, 128, C), BF), "g": ((31, 128, C), BF),
-    "z": ((T, C), BF), "gz": ((T, C), BF), "p": ((T, 3 * C), BF), "att": ((T * HALF, 256), F32), "mixed": ((T, C), BF),
+    "x": ((31, 32) + GRID, BF), "g": ((31, 32) + GRID, BF),
+    "z": ((T, C), BF), "gz": ((T, C), BF), "p": ((T, 3 * C), BF), "att": ((T * HALF, 256), BF), "mixed": ((T, C), BF),
     "gres": ((T, C), F32), "bias": ((2, HALF * WROWS, 256), F32), "dbias": ((HALF * WROWS, 256), F32),
-    "acc": ((256, COLS), F32), "small": ((8, C), F32), "small_core": ((8, C), F32), "small_lon": ((8, 8, C), F32),
-    "small_lat": ((8, 8, C), F32), "sent": ((256, COLS), BF), "land_core": ((128, COLS), BF), "part": ((128, COLS), BF),
-    "land_lon": ((8, 16, COLS), BF), "land_lat": ((8, 16, COLS), BF),
-    "side": ((2, 28, 16, C), BF), "foot": ((2, 3, 128, C), BF), "land_side": ((2, 28, 16, C), BF),
-    "land_foot": ((2, 3, 112, C), BF),
+    "rel": ((8, 512), F32), "strip": ((SLAB, 8, 256), F32), "dstrip": ((8, SLAB, 256), F32),
+    "acc": ((256, COLS), F32), "small": ((24, C), F32), "small_core": ((24, C), F32), "small_lon": ((8, 24, C), F32),
+    "small_lat": ((8, 24, C), F32), "sent": ((256, COLS), BF), "land_core": ((128, COLS), BF), "part": ((128, COLS), BF),
+    "land_lon": ((8, 16, COLS), BF), "land_lat": ((8, 16, COLS), BF), "total": ((256, COLS), BF),
+    "side": ((2, 28, 4) + GRID, BF), "foot": ((2, 3, 32) + GRID, BF), "land_side": ((2, 28, 4) + GRID, BF),
+    "land_foot": ((2, 3, 28) + GRID, BF),
+    "tail": ((8, C), F32), "tail_lon": ((16, 8, C), F32), "tail_lat": ((8, 8, C), F32),
 }
-SEMS = (2, 12, 12, 24, 24, 40, 40)
+SEMS = (2, 12, 12, 24, 24, 24, 24, 40, 40, 23, 23)
 
 
 def kernel(*refs):
@@ -491,8 +663,9 @@
     names = INS + tuple(OUTS) + tuple(SCRATCH)
     for name, ref in zip(names, refs):
         setattr(s, name, ref)
-    s.near_sem, h0, h1, a0, a1, b0, b1 = refs[len(names):]
-    s.halo, s.sums = (h0, h1), ((a0, a1), (b0, b1))
+    sems = refs[len(names):]
+    s.near_sem, s.halo, s.tails = sems[0], sems[1:3], sems[9:11]
+    s.sums = (sems[3:5], sems[5:7], sems[7:9])
     s.lat, s.lon = lax.axis_index("lat"), lax.axis_index("lon")
     s.last = s.lat == 7
     compute(s)
@@ -516,21 +689,16 @@
 def local(tokens, out_grad, gains, shifts, w_qkv, b_qkv, w_proj, w_in, w_out, rel_bias):
     rows_n, cols_n, levels, channels = tokens.shape
     scale = float(rows_n * lax.axis_size("lat") * cols_n * lax.axis_size("lon") * levels) ** -0.5
-    index = jnp.asarray(strip_map().reshape(-1))
-    onehot = (index[:, None] == jnp.arange(NREL, dtype=jnp.int32)[None, :]).astype(F32)
-    strip = lax.dot_general(rel_bias, onehot, NT, precision=lax.Precision.HIGHEST).reshape(HEADS, SLAB, 256)
-    pm = jnp.asarray(placement(), BF)
-    flat = (rows_n, cols_n * levels, channels)
-    res, ing, total, small = fused(
-        tokens.reshape(flat), out_grad.reshape(flat), pm, strip, gains, shifts, w_qkv, b_qkv[None], w_proj, w_in, w_out
+    res, ing, o_in, o_out, o_qkv, o_proj, small, tail = fused(
+        tokens, out_grad, jnp.asarray(placement(), BF), jnp.asarray(strip_map()), gains, shifts, w_qkv, b_qkv[None],
+        w_proj, w_in, w_out, rel_bias,
     )
-    total = total.astype(F32) * scale
-    small = small * scale
-    dstrip = total[:, STRIP].reshape(2, HEADS, SLAB, 128).transpose(1, 2, 0, 3).reshape(HEADS, -1)
-    table = lax.dot_general(dstrip, onehot, NN, precision=lax.Precision.HIGHEST)
+    def scaled(value):
+        return value.astype(F32) * scale
+    table = jnp.concatenate([small[0:8], small[8:16]], 1)[:, :NREL]
     return (
-        res.reshape(tokens.shape), ing.reshape(tokens.shape), small[0:2], small[2:4], total[:, W_QKV],
-        small[4:7].reshape(3 * C), total[:, W_PROJ], total[:, W_IN], total[:, W_OUT].T, table,
+        res, ing, scaled(jnp.stack([tail[0], small[19]])), scaled(jnp.stack([tail[1], small[20]])), scaled(o_qkv),
+        scaled(small[16:19].reshape(3 * C)), scaled(o_proj), scaled(o_in), scaled(o_out), scaled(table),
     )
 
 

time: 167 us -> 135 us (0.81)
  Pallas kernels: 137 us -> 120 us
  local copies, waits for them, and re-layouts: 17.3 us -> 6.56 us
  matrix products: 9.13 us -> 0 us
  other arithmetic: 1.68 us -> 7.34 us
    pallas_call x1, Pallas kernels: 137 us -> 120 us  [fused(): pl.pallas_call(kernel, out_shape=tuple((jax.ShapeDtypeStruct(*v) for v in...]
    dot_general x2 -> x0, matrix products: 9.13 us -> none  [the longest x1 5.1 us: local(): lax.dot_general(rel_bias, onehot, NT, precision=lax.Precision.HIGHEST)]
    reshape x7 -> x0, local copies, waits for them, and re-layouts: 8.82 us -> none  [the longest x1 4 us: local(): res.reshape(tokens.shape)]
    mul x2 -> x8, other arithmetic: 1.68 us -> 7.34 us  [scaled(): return value.astype(F32) * scale]
where the time goes in v3:
time: 135 us; the launch traced here: 134 us
  Pallas kernels  120 us (89%)
  other arithmetic  7.34 us (5%)
  local copies, waits for them, and re-layouts  6.56 us (5%)
    pallas_call x1, Pallas kernels, fused(): pl.pallas_call(kernel, out_shape=tuple((jax.ShapeDtypeStruct(*v) for v in...  120 us
    mul x8, other arithmetic, scaled(): return value.astype(F32) * scale  7.34 us
    unnamed x12, local copies, waits for them, and re-layouts  3.17 us

profile of v3, /device:TPU:1, one launch (start us, length us, event | category | flops | bytes accessed | tf_op | source)
XLA Modules:
  0.0 134.3 jit_solution(10993308039671495912)
XLA Ops:
  0.6 1.3 broadcast_in_dim.3.refs_7_
  1.9 119.7 %windows.1 = (bf16[28,28,4,256]{3,2,1,0:T(4,128)(2,1)}, bf16[28,28,4,256]{3,2,1,0:T(4,128)(2,1)}, bf16[256,1024]{1,0:T(8,128)(2,1)}, bf16[1024,256]{1,0:T(8,128)...) custom-call(bf16[28,28,4,256]{3,2,1,0:T(4,128)(2,1)} %refs_0_.1, ...), custom_call_target="tpu_custom_call" | custom-call | tf_op jit(solution)/shard_map/windows/pallas_call | solution.py:676
  121.7 0.0 copy-start.2
  121.7 0.8 fusion.2
  122.5 0.6 maximum_multiply_fusion.1
  123.1 0.6 maximum_multiply_fusion
  123.7 0.7 fusion.1
  124.4 0.0 copy-start.3
  124.4 0.6 fusion
  125.0 0.7 slice_multiply_fusion
  125.7 0.6 mul.51
  126.3 2.1 %convert_multiply_fusion = f32[1024,256]{1,0:T(8,128)} fusion(bf16[1024,256]{1,0:T(8,128)(2,1)} %get-tuple-element.25), kind=kLoop, calls=%fused_computation | loop fusion | flops 524288 | bytes 1572864 | tf_op jit(solution)/shard_map/mul | solution.py:697
  128.4 0.0 copy-start.4
  128.4 0.0 copy-start.1
  128.4 0.0 copy-done.2
  128.4 1.1 convert_multiply_fusion.1
  129.5 0.0 copy-done.3
  129.5 0.9 convert_multiply_fusion.2
  130.4 0.0 copy-done.4
  130.4 0.7 convert_multiply_fusion.3
  131.2 0.0 copy-done.1
  131.2 1.2 copy.24
  132.3 0.8 copy-done
  133.2 1.2 copy.25
  (1 shorter events, 0.0 us)
Async XLA Ops:
  121.7 6.7 %copy-start.2 = (bf16[256,1024]{1,0:T(8,128)(2,1)S(1)}, bf16[256,1024]{1,0:T(8,128)(2,1)}, u32[]{:S(2)}) copy-start(bf16[256,1024]{1,0:T(8,128)(2,1)} %get-tuple-element.24) | copy-start | bytes 1572868
  124.4 5.1 %copy-start.3 = (bf16[256,768]{1,0:T(8,128)(2,1)S(1)}, bf16[256,768]{1,0:T(8,128)(2,1)}, u32[]{:S(2)}) copy-start(bf16[256,768]{1,0:T(8,128)(2,1)} %get-tuple-element.22) | copy-start | bytes 1179652
  128.4 2.0 %copy-start.4 = (bf16[256,256]{1,0:T(8,128)(2,1)S(1)}, bf16[256,256]{1,0:T(8,128)(2,1)}, u32[]{:S(2)}) copy-start(bf16[256,256]{1,0:T(8,128)(2,1)} %get-tuple-element.23) | copy-start | bytes 393220
  128.4 2.8 %copy-start.1 = (bf16[28,28,4,256]{3,2,1,0:T(4,128)(2,1)S(1)}, bf16[28,28,4,256]{3,2,1,0:T(4,128)(2,1)}, u32[]{:S(2)}) copy-start(bf16[28,28,4,256]{3,2,1,0:T(4,128)(2,1)} %get-tuple-element.44) | copy-start | bytes 4816900
  131.2 2.0 %copy-start = (bf16[28,28,4,256]{3,2,1,0:T(4,128)(2,1)S(1)}, bf16[28,28,4,256]{3,2,1,0:T(4,128)(2,1)}, u32[]{:S(2)}) copy-start(bf16[28,28,4,256]{3,2,1,0:T(4,128)(2,1)} %get-tuple-element.45) | copy-start | bytes 4816900

commit v4 on v3

--- a/solution.py
+++ b/solution.py
@@ -76,10 +76,9 @@
     c1 = np.float32(0.044715 * np.sqrt(2.0 / np.pi))
     p2 = p * p
     t = jnp.tanh(p * (c0 + c1 * p2))
-    h = 0.5 * p
     half = 0.5 + 0.5 * t
     act = p * half
-    slope = half + h * (1.0 - t * t) * (c0 + (3.0 * c1) * p2)
+    slope = half + act * (1.0 - half) * ((2.0 * c0) + (6.0 * c1) * p2)
     return act, slope
 
 
@@ -116,9 +115,9 @@
     return jnp.concatenate(parts, 0).T[:WROWS]
 
 
-FIRST, SECOND, LATE = (0, 1024), (1024, 2304), (2304, 3072)
-W_IN, W_PROJ, W_QKV = slice(0, 1024), slice(2048, 2304), slice(2304, 3072)
-COLS = 3072
+FIRST, LATE = (0, 2304), (2304, 3200)
+W_IN, W_PROJ, W_QKV, SHORT = slice(0, 1024), slice(2048, 2304), slice(2304, 3072), slice(3072, 3200)
+COLS = 3200
 LOG2E = np.float32(1.4426950408889634)
 MESH = pl.DeviceIdType.MESH
 
@@ -174,15 +173,17 @@
         copy.wait()
 
 
-def slab(wr, c, a):
-    return pl.ds(pl.multiple_of((wr * 8 + c) * WROWS + a * SLAB, SLAB), SLAB)
+def slab(r, c):
+    wr = r // WIN
+    slot = jnp.where(wr < 3, wr * 6 + c if c < 6 else 12 + wr * 2 + c, 24 + c)
+    return pl.ds(pl.multiple_of(slot * WROWS + (r % WIN) * SLAB, SLAB), SLAB)
 
 
 def gather_own(s, src, dst):
     def row(r, _):
         y = dot(s.pm[0:96, 0:112], src[r + SHIFT, 0:28].reshape(112, C)).astype(BF)
         for c in range(6):
-            dst[slab(r // WIN, c, r % WIN), :] = y[c * SLAB:(c + 1) * SLAB]
+            dst[slab(r, c), :] = y[c * SLAB:(c + 1) * SLAB]
         return 0
     lax.fori_loop(0, 25, row, 0, unroll=5)
 
@@ -191,13 +192,13 @@
     def row(r, _):
         y = dot(s.pm[96:128], src[r + SHIFT].reshape(128, C)).astype(BF)
         for c in range(2):
-            dst[slab(r // WIN, 6 + c, r % WIN), :] = y[c * SLAB:(c + 1) * SLAB]
+            dst[slab(r, 6 + c), :] = y[c * SLAB:(c + 1) * SLAB]
         return 0
     lax.fori_loop(0, 25, row, 0, unroll=5)
     for r in range(25, 28):
         y = dot(s.pm[...], src[r + SHIFT].reshape(128, C)).astype(BF)
         for c in range(8):
-            dst[slab(r // WIN, c, r % WIN), :] = y[c * SLAB:(c + 1) * SLAB]
+            dst[slab(r, c), :] = y[c * SLAB:(c + 1) * SLAB]
 
 
 def halo_out_copies(s, n):
@@ -210,7 +211,7 @@
 
 
 def grid_row(s, src, r, low, high):
-    y = jnp.concatenate([src[slab(r // WIN, c, r % WIN), :] for c in range(low, high)], 0)
+    y = jnp.concatenate([src[slab(r, c), :] for c in range(low, high)], 0)
     return dot(s.pm[low * SLAB:high * SLAB], y, TN).astype(BF).reshape(32, LEV, C)
 
 
@@ -236,8 +237,8 @@
     scatter_foot(s, src, n)
 
     def row(r, _):
-        y = grid_row(s, src, r, 4, 8)
-        dst[r + SHIFT] = y[:28]
+        y = grid_row(s, src, r, 6, 8)
+        dst[r + SHIFT, 24:28] = y[24:28]
         s.side[n, r + SHIFT] = y[28:]
         return 0
     lax.fori_loop(0, 25, row, 0, unroll=5)
@@ -247,10 +248,7 @@
 
 def scatter_own(s, src, dst):
     def row(r, _):
-        y = grid_row(s, src, r, 0, 4)
-        dst[r + SHIFT, 0:16] = y[:16]
-        seam = dst[r + SHIFT, 16:20].reshape(16, C) + y[16:20].reshape(16, C)
-        dst[r + SHIFT, 16:20] = seam.reshape(4, LEV, C)
+        dst[r + SHIFT, 0:24] = grid_row(s, src, r, 0, 6)[0:24]
         return 0
     lax.fori_loop(0, 25, row, 0, unroll=5)
 
@@ -307,6 +305,9 @@
     table = table[0:8] + table[8:16] + table[16:24]
     s.small[0:8] = table[:, 0:256]
     s.small[8:16] = table[:, 256:512]
+    s.acc[:, SHORT] = jnp.zeros((C, 128), F32)
+    s.acc[0:32, SHORT] = s.small[:, 0:128]
+    s.acc[32:64, SHORT] = s.small[:, 128:256]
 
 
 def tail_lon_copies(s):
@@ -340,12 +341,12 @@
 def tail_done(s):
     for copy in tail_lat_copies(s):
         copy.wait()
-    s.tail_out[...] = sum(s.tail_lat[i] for i in range(8))
+    return sum(s.tail_lat[i] for i in range(8))
 
 
 class Exchange:
-    def __init__(self, s, cols, number, small=False):
-        self.s, self.cols, self.sems, self.small = s, slice(*cols), s.sums[number], small
+    def __init__(self, s, cols, number):
+        self.s, self.cols, self.sems = s, slice(*cols), s.sums[number]
         self.core, self.chip = s.lon % 2, s.lon // 2
         self.half = pl.ds(pl.multiple_of(self.core * 128, 128), 128)
         self.other = pl.ds(pl.multiple_of((1 - self.core) * 128, 128), 128)
@@ -355,8 +356,6 @@
     def core_copies(self):
         s = self.s
         out = [send(s.sent.at[self.other, self.cols], s.land_core.at[:, self.cols], self.sems, 0, self.twin)]
-        if self.small:
-            out.append(send(s.small, s.small_core, self.sems, 24, self.twin))
         return out
 
     def lon_copies(self):
@@ -366,8 +365,6 @@
             to = (s.lat, peer * 2 + self.core)
             rows = pl.ds(pl.multiple_of(peer * 16, 16), 16)
             out.append(send(s.part.at[rows, self.cols], s.land_lon.at[self.chip, :, self.cols], self.sems, d, to))
-            if self.small:
-                out.append(send(s.small_lon.at[self.chip], s.small_lon.at[self.chip], self.sems, 24 + d, to))
         return out
 
     def lat_copies(self):
@@ -376,8 +373,6 @@
             to = ((s.lat + d) % 8, s.lon)
             mine = s.land_lat.at[s.lat, :, self.cols]
             out.append(send(mine, mine, self.sems, 8 + d, to))
-            if self.small:
-                out.append(send(s.small_lat.at[s.lat], s.small_lat.at[s.lat], self.sems, 32 + d, to))
         return out
 
     def gather_copies(self):
@@ -405,8 +400,6 @@
         both = s.acc[self.half, self.cols] + s.land_core[:, self.cols].astype(F32)
         s.acc[self.half, self.cols] = both
         s.part[:, self.cols] = both.astype(BF)
-        if self.small:
-            s.small_lon[self.chip] = s.small[...] + s.small_core[...]
         for copy in self.lon_copies():
             copy.start()
 
@@ -418,8 +411,6 @@
         for d in range(1, 8):
             total += s.land_lon[(self.chip + d) % 8, :, self.cols].astype(F32)
         s.land_lat[s.lat, :, self.cols] = total.astype(BF)
-        if self.small:
-            s.small_lat[s.lat] = sum(s.small_lon[i] for i in range(8))
         for copy in self.lat_copies():
             copy.start()
 
@@ -431,8 +422,6 @@
         for i in range(1, 8):
             total += s.land_lat[i, :, self.cols].astype(F32)
         s.total[self.share, self.cols] = total.astype(BF)
-        if self.small:
-            s.small_out[...] = sum(s.small_lat[i] for i in range(8))
         for copy in self.gather_copies():
             copy.start()
 
@@ -447,7 +436,7 @@
             copy.wait()
 
 
-def compute(s, chunk_windows=4):
+def compute(s, chunk_windows=8):
     pair, group = head_masks()
     scale = np.float32(HD ** -0.5)
     CH = chunk_windows * WROWS
@@ -502,8 +491,8 @@
         s.mixed[rows, :] = down_keys(vt, jnp.concatenate(lows, 0)).astype(BF)
 
     def phase_a(step, _):
-        i = jnp.where(step < 3, 2 * step, jnp.where(step < 6, 2 * step - 5, step))
-        pl.when(step == 3)(rest)
+        i = step
+        pl.when(step == 2)(rest)
         rows = pl.ds(pl.multiple_of(i * CH, CH), CH)
         x = s.z[rows, :].astype(F32)
         _, _, hidden1 = layer_norm(x, s.gains[0:1], s.shifts[0:1])
@@ -541,13 +530,12 @@
         s.mixed[rows, :] = dot(low, s.w_proj[...], NT).astype(BF)
         return 0
 
-    lax.fori_loop(0, 8, phase_a, 0)
+    lax.fori_loop(0, 4, phase_a, 0)
     for f in range(4):
         cols = slice(1024 + f * 256, 1280 + f * 256)
         s.acc[:, cols] = s.acc[:, cols].T
-    first, second, late = Exchange(s, FIRST, 0), Exchange(s, SECOND, 1), Exchange(s, LATE, 2, small=True)
+    first, late = Exchange(s, FIRST, 0), Direct(s, LATE, 2)
     first.core_start()
-    second.core_start()
     scatter_all(s, s.gz, s.res, 0)
 
     def backward_window(w):
@@ -575,12 +563,8 @@
 
     def phase_b(i, _):
         rows = pl.ds(pl.multiple_of(i * CH, CH), CH)
-        steps = (
-            first.lon_start, second.lon_start, first.lat_start, second.lat_start,
-            first.gather_start, second.gather_start, first.pair_start,
-        )
-        for at, step in enumerate(steps):
-            pl.when(i == at + 1)(step)
+        for at, step in ((1, first.lon_start), (2, first.lat_start), (3, first.gather_start)):
+            pl.when(i == at)(step)
 
         def win(w, _):
             for u in range(4):
@@ -595,15 +579,15 @@
             s.small[16 + part:17 + part] += sums[:, part * C:(part + 1) * C]
         return 0
 
-    lax.fori_loop(0, 8, phase_b, 0)
+    lax.fori_loop(0, 4, phase_b, 0)
     collect_table(s)
-    late.core_start()
+    late.lon_start()
     halo_out_done(s, s.res, 0)
 
     def phase_c(step, _):
-        i = jnp.where(step < 2, 7 - step, jnp.where(step < 5, 9 - 2 * step, 14 - 2 * step))
+        i = 3 - step
         for at, action in (
-            (2, late.lon_start), (3, second.pair_start), (5, lambda: scatter_sent(s, s.z, s.ing, 1)), (6, late.lat_start),
+            (1, first.pair_start), (2, lambda: scatter_sent(s, s.z, s.ing, 1)), (3, late.lat_start),
         ):
             pl.when(step == at)(action)
         rows = pl.ds(pl.multiple_of(i * CH, CH), CH)
@@ -614,22 +598,95 @@
         s.z[rows, :] = (s.gres[rows, :] + norm_backward(gh, xhat, istd, s.gains[0:1])).astype(BF)
         return 0
 
-    lax.fori_loop(0, 8, phase_c, 0)
+    lax.fori_loop(0, 4, phase_c, 0)
     tail_lon_start(s)
+    late.gather_start()
     scatter_own(s, s.z, s.ing)
-    late.gather_start()
     tail_lat_start(s)
     first.pair_done()
-    second.pair_done()
-    s.o_in[...] = s.total[:, W_IN]
+    def scaled(value):
+        return value.astype(F32) * s.scale
+
+    s.o_in[...] = scaled(s.total[:, W_IN])
     for f in range(4):
-        s.o_out[f * 256:(f + 1) * 256] = s.total[:, 1024 + f * 256:1280 + f * 256]
-    s.o_proj[...] = s.total[:, W_PROJ]
+        s.o_out[f * 256:(f + 1) * 256] = scaled(s.total[:, 1024 + f * 256:1280 + f * 256])
+    s.o_proj[...] = scaled(s.total[:, W_PROJ])
     halo_out_done(s, s.ing, 1)
-    late.pair_start()
-    tail_done(s)
-    late.pair_done()
-    s.o_qkv[...] = s.total[:, W_QKV]
+    late.done()
+    s.o_qkv[...] = scaled(s.total[:, W_QKV])
+    short = [scaled(s.total[0:32, SHORT]), scaled(s.total[32:64, SHORT])]
+    for side in range(2):
+        lanes = slice(side * 128, side * 128 + 128)
+        s.o_table[:, lanes] = short[side][0:8]
+        s.o_gains[1:2, lanes] = short[side][19:20]
+        s.o_shifts[1:2, lanes] = short[side][20:21]
+        for part in range(3):
+            s.o_bias[part * C + side * 128:part * C + side * 128 + 128] = short[side][16 + part]
+    s.o_table[:, 256:384] = short[0][8:16]
+    s.o_table[:, 384:NREL] = short[1][8:16][:, :NREL - 384]
+    tail = tail_done(s) * s.scale
+    s.o_gains[0:1] = tail[0:1]
+    s.o_shifts[0:1] = tail[1:2]
+
+
+class Direct:
+    def __init__(self, s, cols, number):
+        self.s, self.cols, self.sems = s, slice(*cols), s.sums[number]
+        self.share = pl.ds(pl.multiple_of(s.lon * 16, 16), 16)
+
+    def lon_copies(self):
+        s, out = self.s, []
+        for d in range(1, 16):
+            peer = (s.lon + d) % 16
+            rows = pl.ds(pl.multiple_of(peer * 16, 16), 16)
+            out.append(send(s.sent.at[rows, self.cols], s.land_late.at[s.lon], self.sems, d, (s.lat, peer)))
+        return out
+
+    def lat_copies(self):
+        s, out = self.s, []
+        mine = s.land_lat.at[s.lat, :, self.cols]
+        for d in range(1, 8):
+            out.append(send(mine, mine, self.sems, 15 + d, ((s.lat + d) % 8, s.lon)))
+        return out
+
+    def gather_copies(self):
+        s, out = self.s, []
+        mine = s.total.at[self.share, self.cols]
+        for d in range(1, 16):
+            out.append(send(mine, mine, self.sems, 22 + d, (s.lat, (s.lon + d) % 16)))
+        return out
+
+    def lon_start(self):
+        s = self.s
+        s.sent[:, self.cols] = s.acc[:, self.cols].astype(BF)
+        for copy in self.lon_copies():
+            copy.start()
+
+    def lat_start(self):
+        s = self.s
+        for copy in self.lon_copies():
+            copy.wait()
+        total = s.acc[self.share, self.cols]
+        for d in range(1, 16):
+            total += s.land_late[(s.lon + d) % 16].astype(F32)
+        s.land_lat[s.lat, :, self.cols] = total.astype(BF)
+        for copy in self.lat_copies():
+            copy.start()
+
+    def gather_start(self):
+        s = self.s
+        for copy in self.lat_copies():
+            copy.wait()
+        total = s.land_lat[0, :, self.cols].astype(F32)
+        for i in range(1, 8):
+            total += s.land_lat[i, :, self.cols].astype(F32)
+        s.total[self.share, self.cols] = total.astype(BF)
+        for copy in self.gather_copies():
+            copy.start()
+
+    def done(self):
+        for copy in self.gather_copies():
+            copy.wait()
 
 
 class Refs:
@@ -640,25 +697,25 @@
 GRID = (LEV, C)
 INS = ("x_in", "g_in", "pm", "index", "gains", "shifts", "w_qkv", "b_qkv", "w_proj", "w_in", "w_out", "rel_bias")
 OUTS = {
-    "res": ((28, 28) + GRID, BF), "ing": ((28, 28) + GRID, BF), "o_in": ((C, FF), BF), "o_out": ((FF, C), BF),
-    "o_qkv": ((C, 3 * C), BF), "o_proj": ((C, C), BF), "small_out": ((24, C), F32), "tail_out": ((8, C), F32),
+    "res": ((28, 28) + GRID, BF), "ing": ((28, 28) + GRID, BF), "o_gains": ((2, C), F32), "o_shifts": ((2, C), F32),
+    "o_qkv": ((C, 3 * C), F32), "o_bias": ((3 * C,), F32), "o_proj": ((C, C), F32), "o_in": ((C, FF), F32),
+    "o_out": ((FF, C), F32), "o_table": ((HEADS, NREL), F32),
 }
 SCRATCH = {
     "x": ((31, 32) + GRID, BF), "g": ((31, 32) + GRID, BF),
     "z": ((T, C), BF), "gz": ((T, C), BF), "p": ((T, 3 * C), BF), "att": ((T * HALF, 256), BF), "mixed": ((T, C), BF),
     "gres": ((T, C), F32), "bias": ((2, HALF * WROWS, 256), F32), "dbias": ((HALF * WROWS, 256), F32),
     "rel": ((8, 512), F32), "strip": ((SLAB, 8, 256), F32), "dstrip": ((8, SLAB, 256), F32),
-    "acc": ((256, COLS), F32), "small": ((24, C), F32), "small_core": ((24, C), F32), "small_lon": ((8, 24, C), F32),
-    "small_lat": ((8, 24, C), F32), "sent": ((256, COLS), BF), "land_core": ((128, COLS), BF), "part": ((128, COLS), BF),
+    "acc": ((256, COLS), F32), "small": ((32, C), F32), "land_late": ((16, 16, 896), BF), "sent": ((256, COLS), BF), "land_core": ((128, COLS), BF), "part": ((128, COLS), BF),
     "land_lon": ((8, 16, COLS), BF), "land_lat": ((8, 16, COLS), BF), "total": ((256, COLS), BF),
     "side": ((2, 28, 4) + GRID, BF), "foot": ((2, 3, 32) + GRID, BF), "land_side": ((2, 28, 4) + GRID, BF),
     "land_foot": ((2, 3, 28) + GRID, BF),
     "tail": ((8, C), F32), "tail_lon": ((16, 8, C), F32), "tail_lat": ((8, 8, C), F32),
 }
-SEMS = (2, 12, 12, 24, 24, 24, 24, 40, 40, 23, 23)
-
-
-def kernel(*refs):
+SEMS = (2, 12, 12, 24, 24, 24, 24, 38, 38, 23, 23)
+
+
+def kernel(scale, *refs):
     s = Refs()
     names = INS + tuple(OUTS) + tuple(SCRATCH)
     for name, ref in zip(names, refs):
@@ -667,14 +724,14 @@
     s.near_sem, s.halo, s.tails = sems[0], sems[1:3], sems[9:11]
     s.sums = (sems[3:5], sems[5:7], sems[7:9])
     s.lat, s.lon = lax.axis_index("lat"), lax.axis_index("lon")
-    s.last = s.lat == 7
+    s.last, s.scale = s.lat == 7, scale
     compute(s)
 
 
-def fused(*args):
+def fused(scale, *args):
     vm = pl.BlockSpec(memory_space=pltpu.VMEM)
     return pl.pallas_call(
-        kernel,
+        functools.partial(kernel, scale),
         out_shape=tuple(jax.ShapeDtypeStruct(*v) for v in OUTS.values()),
         in_specs=[pl.BlockSpec(memory_space=pl.ANY)] * 2 + [vm] * (len(INS) - 2),
         out_specs=[vm] * len(OUTS),
@@ -686,20 +743,41 @@
     )(*args)
 
 
+def deliver(arrays):
+    count = len(arrays)
+
+    def body(*refs):
+        ins, outs, held, sems = refs[:count], refs[count:2 * count], refs[2 * count:3 * count], refs[3 * count]
+        come = [pltpu.make_async_copy(ins[i], held[i], sems.at[0, i]) for i in range(count)]
+        leave = [pltpu.make_async_copy(held[i], outs[i], sems.at[1, i]) for i in range(count)]
+        for copy in come:
+            copy.start()
+        for i in range(count):
+            come[i].wait()
+            leave[i].start()
+        for copy in leave:
+            copy.wait()
+
+    some = pl.BlockSpec(memory_space=pl.ANY)
+    return pl.pallas_call(
+        body,
+        out_shape=tuple(jax.ShapeDtypeStruct(v.shape, v.dtype) for v in arrays),
+        in_specs=[some] * count,
+        out_specs=[some] * count,
+        scratch_shapes=[pltpu.VMEM(v.shape, v.dtype) for v in arrays] + [pltpu.SemaphoreType.DMA((2, count))],
+        compiler_params=pltpu.CompilerParams(vmem_limit_bytes=62 * 1024 * 1024),
+        name="deliver",
+    )(*arrays)
+
+
 def local(tokens, out_grad, gains, shifts, w_qkv, b_qkv, w_proj, w_in, w_out, rel_bias):
     rows_n, cols_n, levels, channels = tokens.shape
     scale = float(rows_n * lax.axis_size("lat") * cols_n * lax.axis_size("lon") * levels) ** -0.5
-    res, ing, o_in, o_out, o_qkv, o_proj, small, tail = fused(
-        tokens, out_grad, jnp.asarray(placement(), BF), jnp.asarray(strip_map()), gains, shifts, w_qkv, b_qkv[None],
+    outs = fused(
+        scale, tokens, out_grad, jnp.asarray(placement(), BF), jnp.asarray(strip_map()), gains, shifts, w_qkv, b_qkv,
         w_proj, w_in, w_out, rel_bias,
     )
-    def scaled(value):
-        return value.astype(F32) * scale
-    table = jnp.concatenate([small[0:8], small[8:16]], 1)[:, :NREL]
-    return (
-        res, ing, scaled(jnp.stack([tail[0], small[19]])), scaled(jnp.stack([tail[1], small[20]])), scaled(o_qkv),
-        scaled(small[16:19].reshape(3 * C)), scaled(o_proj), scaled(o_in), scaled(o_out), scaled(table),
-    )
+    return deliver(outs)
 
 
 def solution(mesh):

time: 135 us -> 122 us (0.904)
  other arithmetic: 7.34 us -> 0 us
  local copies, waits for them, and re-layouts: 6.56 us -> 0 us
    mul x8 -> x0, other arithmetic: 7.34 us -> none  [scaled(): return value.astype(F32) * scale]
    unnamed x12 -> x0, local copies, waits for them, and re-layouts: 3.17 us -> none
    slice x2 -> x0, local copies, waits for them, and re-layouts: 1.52 us -> none  [the longest x1 0.81 us: local(): small[20]]
    pallas_call x1 -> x2, Pallas kernels: 120 us -> 120 us  [the longest x1 115 us: fused(): pl.pallas_call(functools.partial(kernel, scale), out_shape=tuple((jax.Sha...]
where the time goes in v4:
time: 122 us; the launch traced here: 121 us
  Pallas kernels  120 us (98%)
    pallas_call x1, Pallas kernels, fused(): pl.pallas_call(functools.partial(kernel, scale), out_shape=tuple((jax.Sha...  115 us
    pallas_call x1, Pallas kernels, deliver(): pl.pallas_call(body, out_shape=tuple((jax.ShapeDtypeStruct(v.shape, v.dty...  5.15 us

profile of v4, /device:TPU:1, one launch (start us, length us, event | category | flops | bytes accessed | tf_op | source)
XLA Modules:
  0.0 121.0 jit_solution(4479560104833259215)
XLA Ops:
  0.6 115.1 %windows.1 = (bf16[28,28,4,256]{3,2,1,0:T(4,128)(2,1)}, bf16[28,28,4,256]{3,2,1,0:T(4,128)(2,1)}, f32[2,256]{1,0:T(2,128)}, f32[2,256]{1,0:T(2,128)}, f32[256,76...) custom-call(bf16[28,28,4,256]{3,2,1,0:T(4,128)(2,1)} %refs_0_.1, ...), custom_call_target="tpu_custom_call" | custom-call | tf_op jit(solution)/shard_map/windows/pallas_call | solution.py:733
  115.7 5.1 %deliver.1 = (bf16[28,28,4,256]{3,2,1,0:T(4,128)(2,1)}, bf16[28,28,4,256]{3,2,1,0:T(4,128)(2,1)}, f32[2,256]{1,0:T(2,128)}, f32[2,256]{1,0:T(2,128)}, f32[256,76...) custom-call(bf16[28,28,4,256]{3,2,1,0:T(4,128)(2,1)} %get-tuple-elem, ...), custom_call_target="tpu_custom_call" | custom-call | tf_op jit(solution)/shard_map/deliver/pallas_call | solution.py:762

commit v5 on v4

--- a/solution.py
+++ b/solution.py
@@ -185,7 +185,7 @@
         for c in range(6):
             dst[slab(r, c), :] = y[c * SLAB:(c + 1) * SLAB]
         return 0
-    lax.fori_loop(0, 25, row, 0, unroll=5)
+    lax.fori_loop(0, 25, row, 0, unroll=25)
 
 
 def gather_rest(s, src, dst):
@@ -194,7 +194,7 @@
         for c in range(2):
             dst[slab(r, 6 + c), :] = y[c * SLAB:(c + 1) * SLAB]
         return 0
-    lax.fori_loop(0, 25, row, 0, unroll=5)
+    lax.fori_loop(0, 25, row, 0, unroll=25)
     for r in range(25, 28):
         y = dot(s.pm[...], src[r + SHIFT].reshape(128, C)).astype(BF)
         for c in range(8):
@@ -228,7 +228,7 @@
         dst[r + SHIFT] = y[:28]
         s.side[n, r + SHIFT] = y[28:]
         return 0
-    lax.fori_loop(0, 25, row, 0, unroll=5)
+    lax.fori_loop(0, 25, row, 0, unroll=25)
     for copy in halo_out_copies(s, n):
         copy.start()
 
@@ -241,7 +241,7 @@
         dst[r + SHIFT, 24:28] = y[24:28]
         s.side[n, r + SHIFT] = y[28:]
         return 0
-    lax.fori_loop(0, 25, row, 0, unroll=5)
+    lax.fori_loop(0, 25, row, 0, unroll=25)
     for copy in halo_out_copies(s, n):
         copy.start()
 
@@ -250,7 +250,7 @@
     def row(r, _):
         dst[r + SHIFT, 0:24] = grid_row(s, src, r, 0, 6)[0:24]
         return 0
-    lax.fori_loop(0, 25, row, 0, unroll=5)
+    lax.fori_loop(0, 25, row, 0, unroll=25)
 
 
 def halo_out_done(s, dst, n):
@@ -262,7 +262,7 @@
         both = dst[r, 0:4].reshape(16, C) + s.land_side[n, r].reshape(16, C)
         dst[r, 0:4] = both.reshape(4, LEV, C)
         return 0
-    lax.fori_loop(0, 28, row, 0, unroll=7)
+    lax.fori_loop(0, 28, row, 0, unroll=28)
 
 
 def thirds(value):
@@ -492,17 +492,17 @@
 
     def phase_a(step, _):
         i = step
-        pl.when(step == 2)(rest)
-        rows = pl.ds(pl.multiple_of(i * CH, CH), CH)
+        pl.when(step == 1)(rest)
+        rows = pl.ds(pl.multiple_of(i * (2 * CH), CH), 2 * CH)
         x = s.z[rows, :].astype(F32)
         _, _, hidden1 = layer_norm(x, s.gains[0:1], s.shifts[0:1])
         s.p[rows, :] = (dot(hidden1, s.w_qkv[...]) + s.b_qkv[...]).astype(BF)
 
         def win(w, _):
             for u in range(4):
-                forward_window(i * chunk_windows + 4 * w + u)
+                forward_window(i * (2 * chunk_windows) + 4 * w + u)
             return 0
-        lax.fori_loop(0, chunk_windows // 4, win, 0)
+        lax.fori_loop(0, 4, win, 0)
 
         mixed = s.mixed[rows, :]
         resid = s.z[rows, :].astype(F32) + dot(mixed, s.w_proj[...])
@@ -530,7 +530,7 @@
         s.mixed[rows, :] = dot(low, s.w_proj[...], NT).astype(BF)
         return 0
 
-    lax.fori_loop(0, 4, phase_a, 0)
+    lax.fori_loop(0, 2, phase_a, 0)
     for f in range(4):
         cols = slice(1024 + f * 256, 1280 + f * 256)
         s.acc[:, cols] = s.acc[:, cols].T
@@ -583,6 +583,7 @@
     collect_table(s)
     late.lon_start()
     halo_out_done(s, s.res, 0)
+    s.leave["res"].start()
 
     def phase_c(step, _):
         i = 3 - step
@@ -611,9 +612,13 @@
     for f in range(4):
         s.o_out[f * 256:(f + 1) * 256] = scaled(s.total[:, 1024 + f * 256:1280 + f * 256])
     s.o_proj[...] = scaled(s.total[:, W_PROJ])
+    for name in ("o_in", "o_out", "o_proj"):
+        s.leave[name].start()
     halo_out_done(s, s.ing, 1)
+    s.leave["ing"].start()
     late.done()
     s.o_qkv[...] = scaled(s.total[:, W_QKV])
+    s.leave["o_qkv"].start()
     short = [scaled(s.total[0:32, SHORT]), scaled(s.total[32:64, SHORT])]
     for side in range(2):
         lanes = slice(side * 128, side * 128 + 128)
@@ -627,6 +632,8 @@
     tail = tail_done(s) * s.scale
     s.o_gains[0:1] = tail[0:1]
     s.o_shifts[0:1] = tail[1:2]
+    for name in BIG:
+        s.leave[name].wait()
 
 
 class Direct:
@@ -712,7 +719,10 @@
     "land_foot": ((2, 3, 28) + GRID, BF),
     "tail": ((8, C), F32), "tail_lon": ((16, 8, C), F32), "tail_lat": ((8, 8, C), F32),
 }
-SEMS = (2, 12, 12, 24, 24, 24, 24, 38, 38, 23, 23)
+SEMS = (2, 12, 12, 24, 24, 24, 24, 38, 38, 23, 23, 6)
+
+
+BIG = ("res", "ing", "o_qkv", "o_proj", "o_in", "o_out")
 
 
 def kernel(scale, *refs):
@@ -720,7 +730,12 @@
     names = INS + tuple(OUTS) + tuple(SCRATCH)
     for name, ref in zip(names, refs):
         setattr(s, name, ref)
-    sems = refs[len(names):]
+    held = refs[len(names):len(names) + len(BIG)]
+    s.leave = {}
+    sems = refs[len(names) + len(BIG):]
+    for i, name in enumerate(BIG):
+        s.leave[name] = pltpu.make_async_copy(held[i], getattr(s, name), sems[11].at[i])
+        setattr(s, name, held[i])
     s.near_sem, s.halo, s.tails = sems[0], sems[1:3], sems[9:11]
     s.sums = (sems[3:5], sems[5:7], sems[7:9])
     s.lat, s.lon = lax.axis_index("lat"), lax.axis_index("lon")
@@ -734,8 +749,8 @@
         functools.partial(kernel, scale),
         out_shape=tuple(jax.ShapeDtypeStruct(*v) for v in OUTS.values()),
         in_specs=[pl.BlockSpec(memory_space=pl.ANY)] * 2 + [vm] * (len(INS) - 2),
-        out_specs=[vm] * len(OUTS),
-        scratch_shapes=[pltpu.VMEM(*v) for v in SCRATCH.values()] + [pltpu.SemaphoreType.DMA((n,)) for n in SEMS],
+        out_specs=[pl.BlockSpec(memory_space=pl.ANY) if name in BIG else vm for name in OUTS],
+        scratch_shapes=[pltpu.VMEM(*v) for v in SCRATCH.values()] + [pltpu.VMEM(*OUTS[name]) for name in BIG] + [pltpu.SemaphoreType.DMA((n,)) for n in SEMS],
         compiler_params=pltpu.CompilerParams(
             vmem_limit_bytes=63 * 1024 * 1024, collective_id=0, has_side_effects=True
         ),

time: 122 us -> 116 us (0.951)
  Pallas kernels: 120 us -> 115 us
    pallas_call x1, Pallas kernels: 115 us -> 110 us  [fused(): pl.pallas_call(functools.partial(kernel, scale), out_shape=tuple((jax.Sha...]
where the time goes in v5:
time: 116 us
  Pallas kernels  115 us (99%)
    pallas_call x1, Pallas kernels, fused(): pl.pallas_call(functools.partial(kernel, scale), out_shape=tuple((jax.Sha...  110 us
    pallas_call x1, Pallas kernels, deliver(): pl.pallas_call(body, out_shape=tuple((jax.ShapeDtypeStruct(v.shape, v.dty...  5.15 us

profile of v5, /device:TPU:1, one launch (start us, length us, event | category | flops | bytes accessed | tf_op | source)
XLA Modules:
  0.0 115.9 jit_solution(15005388492232208769)
XLA Ops:
  0.6 109.9 %windows.1 = (bf16[28,28,4,256]{3,2,1,0:T(4,128)(2,1)}, bf16[28,28,4,256]{3,2,1,0:T(4,128)(2,1)}, f32[2,256]{1,0:T(2,128)}, f32[2,256]{1,0:T(2,128)}, f32[256,76...) custom-call(bf16[28,28,4,256]{3,2,1,0:T(4,128)(2,1)} %refs_0_.1, ...), custom_call_target="tpu_custom_call" | custom-call | tf_op jit(solution)/shard_map/windows/pallas_call | solution.py:748
  110.6 5.1 %deliver.1 = (bf16[28,28,4,256]{3,2,1,0:T(4,128)(2,1)}, bf16[28,28,4,256]{3,2,1,0:T(4,128)(2,1)}, f32[2,256]{1,0:T(2,128)}, f32[2,256]{1,0:T(2,128)}, f32[256,76...) custom-call(bf16[28,28,4,256]{3,2,1,0:T(4,128)(2,1)} %get-tuple-elem, ...), custom_call_target="tpu_custom_call" | custom-call | tf_op jit(solution)/shard_map/deliver/pallas_call | solution.py:777

commit v6 on v5

--- a/solution.py
+++ b/solution.py
@@ -129,13 +129,9 @@
     )
 
 
-def greet(s):
-    barrier = pltpu.get_barrier_semaphore()
+def greet_peers(s):
     peers = [((s.lat + d) % 8, s.lon) for d in range(1, 8)] + [(s.lat, (s.lon + d) % 16) for d in range(1, 16)]
-    peers += [((s.lat + d) % 8, (s.lon + d) % 16) for d in (1, -1)]
-    for peer in peers:
-        pl.semaphore_signal(barrier, inc=1, device_id=peer, device_id_type=MESH)
-    pl.semaphore_wait(barrier, len(peers))
+    return peers + [((s.lat + d) % 8, (s.lon + d) % 16) for d in (1, -1)]
 
 
 def near_copies(s):
@@ -155,10 +151,16 @@
     return far
 
 
+def enter(s):
+    for copy in near_copies(s) + s.weights:
+        copy.start()
+    barrier = pltpu.get_barrier_semaphore()
+    for peer in greet_peers(s):
+        pl.semaphore_signal(barrier, inc=1, device_id=peer, device_id_type=MESH)
+
+
 def halo_start(s):
-    for copy in near_copies(s):
-        copy.start()
-    greet(s)
+    pl.semaphore_wait(pltpu.get_barrier_semaphore(), len(greet_peers(s)))
     for copy in halo_in_copies(s):
         copy.start()
 
@@ -442,7 +444,7 @@
     CH = chunk_windows * WROWS
     nwin = 32
 
-    halo_start(s)
+    enter(s)
 
     expand_table(s)
     key_row = lax.broadcasted_iota(jnp.int32, (WROWS, 256), 0)
@@ -467,6 +469,9 @@
     near_done(s)
     for src, dst in ((s.x, s.z), (s.g, s.gz)):
         gather_own(s, src, dst)
+    halo_start(s)
+    for copy in s.weights:
+        copy.wait()
 
     def rest():
         halo_in_done(s)
@@ -719,9 +724,10 @@
     "land_foot": ((2, 3, 28) + GRID, BF),
     "tail": ((8, C), F32), "tail_lon": ((16, 8, C), F32), "tail_lat": ((8, 8, C), F32),
 }
-SEMS = (2, 12, 12, 24, 24, 24, 24, 38, 38, 23, 23, 6)
-
-
+SEMS = (2, 12, 12, 24, 24, 24, 24, 38, 38, 23, 23, 6, 4)
+
+
+WEIGHTS = {"w_qkv": ((C, 3 * C), BF), "w_proj": ((C, C), BF), "w_in": ((C, FF), BF), "w_out": ((FF, C), BF)}
 BIG = ("res", "ing", "o_qkv", "o_proj", "o_in", "o_out")
 
 
@@ -732,7 +738,12 @@
         setattr(s, name, ref)
     held = refs[len(names):len(names) + len(BIG)]
     s.leave = {}
-    sems = refs[len(names) + len(BIG):]
+    local_weights = refs[len(names) + len(BIG):len(names) + len(BIG) + len(WEIGHTS)]
+    sems = refs[len(names) + len(BIG) + len(WEIGHTS):]
+    s.weights = []
+    for i, name in enumerate(WEIGHTS):
+        s.weights.append(pltpu.make_async_copy(getattr(s, name), local_weights[i], sems[12].at[i]))
+        setattr(s, name, local_weights[i])
     for i, name in enumerate(BIG):
         s.leave[name] = pltpu.make_async_copy(held[i], getattr(s, name), sems[11].at[i])
         setattr(s, name, held[i])
@@ -748,9 +759,13 @@
     return pl.pallas_call(
         functools.partial(kernel, scale),
         out_shape=tuple(jax.ShapeDtypeStruct(*v) for v in OUTS.values()),
-        in_specs=[pl.BlockSpec(memory_space=pl.ANY)] * 2 + [vm] * (len(INS) - 2),
+        in_specs=[
+            pl.BlockSpec(memory_space=pl.ANY) if name in WEIGHTS or name in ("x_in", "g_in") else vm for name in INS
+        ],
         out_specs=[pl.BlockSpec(memory_space=pl.ANY) if name in BIG else vm for name in OUTS],
-        scratch_shapes=[pltpu.VMEM(*v) for v in SCRATCH.values()] + [pltpu.VMEM(*OUTS[name]) for name in BIG] + [pltpu.SemaphoreType.DMA((n,)) for n in SEMS],
+        scratch_shapes=[pltpu.VMEM(*v) for v in SCRATCH.values()] + [pltpu.VMEM(*OUTS[name]) for name in BIG] + [
+            pltpu.VMEM(*v) for v in WEIGHTS.values()
+        ] + [pltpu.SemaphoreType.DMA((n,)) for n in SEMS],
         compiler_params=pltpu.CompilerParams(
             vmem_limit_bytes=63 * 1024 * 1024, collective_id=0, has_side_effects=True
         ),

time: 116 us -> 112 us (0.966)
  Pallas kernels: 115 us -> 111 us
    pallas_call x1, Pallas kernels: 110 us -> 106 us  [fused(): pl.pallas_call(functools.partial(kernel, scale), out_shape=tuple((jax.Sha...]
where the time goes in v6:
time: 112 us
  Pallas kernels  111 us (99%)
    pallas_call x1, Pallas kernels, fused(): pl.pallas_call(functools.partial(kernel, scale), out_shape=tuple((jax.Sha...  106 us
    pallas_call x1, Pallas kernels, deliver(): pl.pallas_call(body, out_shape=tuple((jax.ShapeDtypeStruct(v.shape, v.dty...  5.15 us

profile of v6, /device:TPU:1, one launch (start us, length us, event | category | flops | bytes accessed | tf_op | source)
XLA Modules:
  0.0 112.2 jit_solution(12802360433149126965)
XLA Ops:
  0.6 106.2 %windows.1 = (bf16[28,28,4,256]{3,2,1,0:T(4,128)(2,1)}, bf16[28,28,4,256]{3,2,1,0:T(4,128)(2,1)}, f32[2,256]{1,0:T(2,128)}, f32[2,256]{1,0:T(2,128)}, f32[256,76...) custom-call(bf16[28,28,4,256]{3,2,1,0:T(4,128)(2,1)} %refs_0_.1, ...), custom_call_target="tpu_custom_call" | custom-call | tf_op jit(solution)/shard_map/windows/pallas_call | solution.py:759
  106.9 5.1 %deliver.1 = (bf16[28,28,4,256]{3,2,1,0:T(4,128)(2,1)}, bf16[28,28,4,256]{3,2,1,0:T(4,128)(2,1)}, f32[2,256]{1,0:T(2,128)}, f32[2,256]{1,0:T(2,128)}, f32[256,76...) custom-call(bf16[28,28,4,256]{3,2,1,0:T(4,128)(2,1)} %get-tuple-elem, ...), custom_call_target="tpu_custom_call" | custom-call | tf_op jit(solution)/shard_map/deliver/pallas_call | solution.py:792

commit v7 on v6

--- a/solution.py
+++ b/solution.py
@@ -593,7 +593,7 @@
     def phase_c(step, _):
         i = 3 - step
         for at, action in (
-            (1, first.pair_start), (2, lambda: scatter_sent(s, s.z, s.ing, 1)), (3, late.lat_start),
+            (1, first.pair_start), (2, lambda: scatter_sent(s, s.z, s.ing, 1)), (2, late.lat_start),
         ):
             pl.when(step == at)(action)
         rows = pl.ds(pl.multiple_of(i * CH, CH), CH)

time: 112 us -> 112 us (level)
  no operation moved by 1% of the time
where the time goes in v7:
time: 112 us
  Pallas kernels  111 us (99%)
    pallas_call x1, Pallas kernels, fused(): pl.pallas_call(functools.partial(kernel, scale), out_shape=tuple((jax.Sha...  106 us
    pallas_call x1, Pallas kernels, deliver(): pl.pallas_call(body, out_shape=tuple((jax.ShapeDtypeStruct(v.shape, v.dty...  5.15 us

profile of v7, /device:TPU:1, one launch (start us, length us, event | category | flops | bytes accessed | tf_op | source)
XLA Modules:
  0.0 112.2 jit_solution(13911868200514700992)
XLA Ops:
  0.6 106.2 %windows.1 = (bf16[28,28,4,256]{3,2,1,0:T(4,128)(2,1)}, bf16[28,28,4,256]{3,2,1,0:T(4,128)(2,1)}, f32[2,256]{1,0:T(2,128)}, f32[2,256]{1,0:T(2,128)}, f32[256,76...) custom-call(bf16[28,28,4,256]{3,2,1,0:T(4,128)(2,1)} %refs_0_.1, ...), custom_call_target="tpu_custom_call" | custom-call | tf_op jit(solution)/shard_map/windows/pallas_call | solution.py:759
  106.8 5.1 %deliver.1 = (bf16[28,28,4,256]{3,2,1,0:T(4,128)(2,1)}, bf16[28,28,4,256]{3,2,1,0:T(4,128)(2,1)}, f32[2,256]{1,0:T(2,128)}, f32[2,256]{1,0:T(2,128)}, f32[256,76...) custom-call(bf16[28,28,4,256]{3,2,1,0:T(4,128)(2,1)} %get-tuple-elem, ...), custom_call_target="tpu_custom_call" | custom-call | tf_op jit(solution)/shard_map/deliver/pallas_call | solution.py:792
